TPU v7x, 128 devices: a whole 4x4x4 slice. The times are simulated.
128 devices in a mesh: dp: 8 (over y_hi, x), ctx: 16 (over z, y_lo, core).
Axes of the slice: x: 4, y: 4 (y_hi: 2, y_lo: 2; y = y_hi * 2 + y_lo), z: 4, core: 2. Of those that a mesh axis runs over, the one named last changes fastest.
Arguments:
- patches: bfloat16 [16384, 1280], P(('dp', 'ctx')), may hold values from -45 to 45
- vision_gain: float32 [1280], replicated, may hold values from 0.25 to 1.75
- vision_bias: float32 [1280], replicated, may hold values from -1.75 to 1.75
- up_weight: bfloat16 [2560, 1280], P(('dp', 'ctx')), may hold values from -0.15625 to 0.15625
- down_weight: bfloat16 [2560, 1280], P(('dp', 'ctx')), may hold values from -0.125 to 0.125
- merge_gain: float32 [1280], replicated, may hold values from 0.25 to 1.75
- merge_bias: float32 [1280], replicated, may hold values from -1.75 to 1.75
- merge_weight: bfloat16 [5120, 8192], P(None, 'dp'), may hold values from -0.078125 to 0.078125
- attn_gain: float32 [8192], replicated, may hold values from 0.25 to 1.75
- query_weight: bfloat16 [8192, 4096], P(None, 'dp'), may hold values from -0.1875 to 0.1875
- kv_weight: bfloat16 [2, 8192, 1024], P(None, None, 'dp'), may hold values from -0.0625 to 0.0625
- text_query: bfloat16 [10240, 4096], P('ctx', 'dp'), may hold values from -120 to 120, as said below
- text_kv: bfloat16 [2, 10240, 1024], P(None, 'ctx', 'dp'), may hold values from -6 to 6, as said below
- doc_ids: int32 [10240], P('ctx'), may hold values from 0 to 3, never falling along the last dimension, each value on 1 to 5120 neighbouring positions
- image_sizes: int32 [128, 4], P(('dp', 'ctx')), may hold values from 1 to 16, as said below
- image_offsets: int32 [128, 4], P(('dp', 'ctx')), may hold values from 0 to 10239, as said below
Outputs:
- context: bfloat16 [10240, 4096], P('ctx', 'dp')
Inputs may be any that keep to these rules, and one draw needn't show every extreme that they name: `image_sizes`: the 4 images of one device hold 32 merged rows together, and one of them holds exactly 16. `image_offsets`: images never intersect; each lies within the 640 positions of one index of ctx; the images of one index of ctx (over all of dp) put at most 32 rows into the positions of one index of ctx, and in every draw some index of ctx takes exactly 32 rows from every index. `text_query`: rows at image positions are not read. `text_kv`: rows at image positions are not read.
All inputs are finite; a program needn't handle non-finite values.
Results may differ from a plain program's by a relative error of at most 0.035.
Values may be sent and summed in bfloat16 or wider, within the bound.
No kernel may reach another device: no remote copies, remote signals or barrier semaphores. Data moves between devices by JAX's collectives and lax.ppermute only.
A program may use at most 128 MiB of HBM per device.

v0:
```python
import math

import jax
import jax.numpy as jnp
from jax import lax
from jax.sharding import PartitionSpec as P

HEAD_DIM = 128
MOST = 16


MASKED_SCORE = -1e30
EPSILON = 1e-06


def layer_norm(rows_in, norm_gain, norm_bias):
    values = rows_in.astype(jnp.float32)
    center = values - jnp.mean(values, axis=-1, keepdims=True)
    spread = jnp.mean(center * center, axis=-1, keepdims=True)
    return (center * lax.rsqrt(spread + EPSILON) * norm_gain + norm_bias).astype(jnp.bfloat16)


def quick_gelu(values):
    return values * jax.nn.sigmoid(1.702 * values)


def rms_scaled(rows_in, norm_gain):
    values = rows_in.astype(jnp.float32)
    mean_square = jnp.mean(values * values, axis=-1, keepdims=True)
    return (values * lax.rsqrt(mean_square + EPSILON) * norm_gain).astype(jnp.bfloat16)


def unit_terms(normed, up_shard, down_shard):
    hidden = lax.dot_general(
        normed, up_shard, (((1,), (1,)), ((), ())), preferred_element_type=jnp.float32
    )
    return jnp.dot(
        quick_gelu(hidden).astype(jnp.bfloat16), down_shard, preferred_element_type=jnp.float32
    )


def row_positions(size_table, offset_table, row_count):
    image_ends = jnp.cumsum(size_table, axis=1, dtype=jnp.int32)
    image_starts = image_ends - size_table
    within = jnp.arange(row_count, dtype=jnp.int32)[None, :, None]
    inside = (within >= image_starts[:, None, :]) & (within < image_ends[:, None, :])
    placed = offset_table[:, None, :] - image_starts[:, None, :] + within
    return jnp.sum(jnp.where(inside, placed, 0), axis=2, dtype=jnp.int32)


def attend(running, queries, key_block, value_block, visible, score_scale):
    row_peak, row_total, accumulated = running
    scores = (
        jnp.einsum("qkgd,tkd->qkgt", queries, key_block, preferred_element_type=jnp.float32)
        * score_scale
    )
    visible_mask = visible[:, None, None, :]
    scores = jnp.where(visible_mask, scores, MASKED_SCORE)
    new_peak = jnp.maximum(row_peak, jnp.max(scores, axis=-1))
    weights = jnp.where(visible_mask, jnp.exp(scores - new_peak[..., None]), 0.0)
    rescale = jnp.exp(row_peak - new_peak)
    row_total = row_total * rescale + jnp.sum(weights, axis=-1)
    blended = jnp.einsum(
        "qkgt,tkd->qkgd",
        weights.astype(jnp.bfloat16),
        value_block,
        preferred_element_type=jnp.float32,
    )
    return (new_peak, row_total, accumulated * rescale[..., None] + blended)


def body(
    patches,
    vision_gain,
    vision_bias,
    up_weight,
    down_weight,
    merge_gain,
    merge_bias,
    merge_weight,
    attn_gain,
    query_weight,
    kv_weight,
    text_query,
    text_kv,
    doc_ids,
    image_sizes,
    image_offsets,
):
    ctx_count = lax.axis_size("ctx")
    ctx_index = lax.axis_index("ctx")
    vision_width = patches.shape[1]
    normed = layer_norm(patches, vision_gain, vision_bias)
    branch = unit_terms(
        normed,
        lax.all_gather(up_weight, ("dp", "ctx"), axis=0, tiled=True),
        lax.all_gather(down_weight, ("dp", "ctx"), axis=0, tiled=True),
    )
    vision = (patches.astype(jnp.float32) + branch).astype(jnp.bfloat16)
    merged_in = layer_norm(vision, merge_gain, merge_bias).reshape(-1, 4 * vision_width)
    positions = row_positions(image_sizes, image_offsets, merged_in.shape[0]).reshape(-1)
    column_in, column_place = (
        lax.all_gather(merged_in, "dp", axis=0, tiled=True),
        lax.all_gather(positions, "dp", axis=0, tiled=True),
    )
    merged = jnp.dot(column_in, merge_weight, preferred_element_type=jnp.float32).astype(
        jnp.bfloat16
    )
    seq_rows = text_query.shape[0]
    capacity = 2 * MOST
    column_size = column_place.shape[0]
    owners = column_place // seq_rows
    one_hot = (owners[:, None] == jnp.arange(ctx_count, dtype=jnp.int32)[None, :]).astype(jnp.int32)
    slot_rank = (
        jnp.sum(jnp.cumsum(one_hot, axis=0, dtype=jnp.int32) * one_hot, axis=1, dtype=jnp.int32) - 1
    )
    slot_index = owners * capacity + slot_rank
    source = (
        jnp.full((ctx_count * capacity,), column_size, jnp.int32)
        .at[slot_index]
        .set(jnp.arange(column_size, dtype=jnp.int32))
    )
    slot_place = jnp.concatenate([column_place, jnp.full((1,), -1, jnp.int32)])[source].reshape(
        ctx_count, capacity
    )
    padded = jnp.concatenate([merged, jnp.zeros((1,) + merged.shape[1:], merged.dtype)], axis=0)
    got_rows = lax.all_to_all(
        padded[source].reshape((ctx_count, capacity) + merged.shape[1:]),
        "ctx",
        split_axis=0,
        concat_axis=0,
        tiled=True,
    )
    got_place = lax.all_to_all(slot_place, "ctx", split_axis=0, concat_axis=0, tiled=True)
    whole_rows = lax.all_gather(got_rows.reshape(-1, merged.shape[1]), "dp", axis=1, tiled=True)
    ready_rows = rms_scaled(whole_rows, attn_gain)
    head_query = jnp.dot(ready_rows, query_weight, preferred_element_type=jnp.float32).astype(
        jnp.bfloat16
    )
    head_pairs = jnp.einsum(
        "rd,sde->sre", ready_rows, kv_weight, preferred_element_type=jnp.float32
    ).astype(jnp.bfloat16)
    image_key = head_pairs[0]
    image_value = head_pairs[1]
    got_place = got_place.reshape(-1)
    slot_total = got_place.shape[0]
    target = jnp.where(got_place >= 0, got_place - ctx_index * seq_rows, seq_rows)
    slot_of = (
        jnp.full((seq_rows,), slot_total, jnp.int32)
        .at[target]
        .set(jnp.arange(slot_total, dtype=jnp.int32), mode="drop")
    )
    is_image = slot_of < slot_total

    def place_rows(text_rows, image_rows):
        padded = jnp.concatenate(
            [image_rows, jnp.zeros((1, image_rows.shape[1]), image_rows.dtype)], axis=0
        )
        return jnp.where(is_image[:, None], padded[slot_of], text_rows)

    queries = place_rows(text_query, head_query)
    key_rows = place_rows(text_kv[0], image_key)
    value_rows = place_rows(text_kv[1], image_value)
    head_width = HEAD_DIM
    key_heads = key_rows.shape[1] // head_width
    group_size = queries.shape[1] // key_rows.shape[1]
    grouped = queries.reshape(seq_rows, key_heads, group_size, head_width)
    query_place = ctx_index * seq_rows + jnp.arange(seq_rows, dtype=jnp.int32)
    score_scale = 1.0 / math.sqrt(head_width)
    initial = (
        jnp.full((seq_rows, key_heads, group_size), MASKED_SCORE, jnp.float32),
        jnp.zeros((seq_rows, key_heads, group_size), jnp.float32),
        jnp.zeros((seq_rows, key_heads, group_size, head_width), jnp.float32),
    )
    running = initial
    key_shard = lax.all_gather(key_rows, "ctx", axis=0, tiled=True)
    value_shard = lax.all_gather(value_rows, "ctx", axis=0, tiled=True)
    doc_shard = lax.all_gather(doc_ids, "ctx", axis=0, tiled=True)
    shard_rows = key_shard.shape[0]
    block_rows = 512
    block_count = shard_rows // block_rows
    key_blocks = key_shard.reshape(block_count, block_rows, key_heads, head_width)
    value_blocks = value_shard.reshape(block_count, block_rows, key_heads, head_width)
    doc_blocks = doc_shard.reshape(block_count, block_rows)

    def key_step(holding, inputs):
        key_block, value_block, doc_block, block_index = inputs
        key_place = block_index * block_rows + jnp.arange(block_rows, dtype=jnp.int32)
        visible = (query_place[:, None] >= key_place[None, :]) & (
            doc_ids[:, None] == doc_block[None, :]
        )
        holding = attend(holding, grouped, key_block, value_block, visible, score_scale)
        return (holding, None)

    running, unused = lax.scan(
        key_step,
        running,
        (key_blocks, value_blocks, doc_blocks, jnp.arange(block_count, dtype=jnp.int32)),
    )
    row_peak, row_total, accumulated = running
    return (accumulated / row_total[..., None]).reshape(seq_rows, -1).astype(jnp.bfloat16)


def solution(mesh):
    return jax.shard_map(
        body,
        mesh=mesh,
        in_specs=(
            P(("dp", "ctx"), None),
            P(),
            P(),
            P(("dp", "ctx"), None),
            P(("dp", "ctx"), None),
            P(),
            P(),
            P(None, "dp"),
            P(),
            P(None, "dp"),
            P(None, None, "dp"),
            P("ctx", "dp"),
            P(None, "ctx", "dp"),
            P("ctx"),
            P(("dp", "ctx"), None),
            P(("dp", "ctx"), None),
        ),
        out_specs=P("ctx", "dp"),
        check_vma=False,
    )
```

profile of v0, /device:TPU:41, one launch (start us, length us, event | category | flops | bytes accessed | tf_op | source)
XLA Modules:
  0.0 902.7 jit_solution(17181244463073114685)
XLA Ops:
  10.4 202.1 %all-gather.18.cloned.1.call-done = bf16[128,20,1280]{2,1,0:T(8,128)(2,1)} async-done(((bf16[1,20,1280]{2,1,0:T(8,128)(2,1)}), bf16[128,20,1280]{2,1,0:T(8,128)(2,1)}) %all-gather.18.cloned.1.call-update) | async-done | bytes 6553616 | tf_op jit(solution)/shard_map/all_gather | solution.py:96
  212.5 10.6 %reshape.413 = bf16[2560,1280]{1,0:T(8,128)(2,1)} reshape(bf16[128,20,1280]{2,1,0:T(8,128)(2,1)} %all-gather.18.cloned.1.call-done) | data formatting | bytes 13107200
  223.1 192.4 %all-gather.20.cloned.1.call-done = bf16[128,20,1280]{2,1,0:T(8,128)(2,1)} async-done(((bf16[1,20,1280]{2,1,0:T(8,128)(2,1)}), bf16[128,20,1280]{2,1,0:T(8,128)(2,1)}) %all-gather.20.cloned.1.call-update) | async-done | bytes 6553616 | tf_op jit(solution)/shard_map/all_gather | solution.py:97
  415.4 10.6 %reshape.415 = bf16[2560,1280]{1,0:T(8,128)(2,1)} reshape(bf16[128,20,1280]{2,1,0:T(8,128)(2,1)} %all-gather.20.cloned.1.call-done) | data formatting | bytes 13107200
  426.1 8.0 fusion.79
  437.4 8.4 all-reduce.4
  448.2 44.6 %all-gather.10.cloned.1.call-done = bf16[256,5120]{1,0:T(8,128)(2,1)} async-done(((bf16[32,5120]{1,0:T(8,128)(2,1)}), bf16[256,5120]{1,0:T(8,128)(2,1)}) %all-gather.10.cloned.1.call-update) | async-done | bytes 2621456 | tf_op jit(solution)/shard_map/all_gather | solution.py:103
  492.8 7.6 convolution_convert_fusion
  502.5 20.4 %all_to_all.14 = bf16[16,32,1024]{2,1,0:T(8,128)(2,1)} all-to-all(bf16[16,32,1024]{2,1,0:T(8,128)(2,1)S(1)} %bitcast.146), channel_id=1, replica_groups=mesh['dp'=8,'ctx'=16] {'ctx'}, dimensions={0} | all-to-all | bytes 2097152 | tf_op jit(solution)/shard_map/all_to_all | solution.py:127
  523.0 3.5 gather_fusion
  527.2 6.2 all-to-all-start
  533.4 3.5 all-to-all-done
  539.7 90.5 %all-gather.12.cloned.1.call-done = bf16[512,8192]{1,0:T(8,128)(2,1)} async-done(((bf16[512,1024]{1,0:T(8,128)(2,1)}), bf16[512,8192]{1,0:T(8,128)(2,1)}) %all-gather.12.cloned.1.call-update) | async-done | bytes 8388624 | tf_op jit(solution)/shard_map/all_gather | solution.py:135
  630.2 5.3 fusion.27
  635.9 4.7 fusion.43
  646.2 16.5 %all-gather = s32[16,1,640]{2,1,0:T(1,128)S(1)} all-gather(s32[1,1,640]{2,1,0:T(1,128)S(1)} %reshape.410), channel_id=1, replica_groups=mesh['dp'=8,'ctx'=16] {'ctx'}, dimensions={0}, use_global_device_ids=true | all-gather | bytes 43520 | tf_op jit(solution)/shard_map/all_gather | solution.py:178
  662.9 10.5 %fusion.37 = bf16[512,512]{1,0:T(8,128)(2,1)S(1)} fusion(bf16[8192,512]{1,0:T(8,128)(2,1)} %param.27, bf16[512,8192]{1,0:T(8,128)(2,1)} %all-gather.12.cloned.1.call-done, f32[8192]{0:T(1024)S(1)} %copy-done.11, f32[512]{0:T(512)S(1)} %add_rsqrt_fusion), kind=kOutput, calls=%fused_computation.53 | convolution fusion | flops 4312006656 | bytes 17336320 | tf_op jit(solution)/shard_map/dot_general | solution.py:137
  673.5 2.8 gather_fusion.3
  679.3 36.7 %all-gather.14.cloned.1.call-done = bf16[10240,128]{1,0:T(8,128)(2,1)} async-done(((bf16[640,128]{1,0:T(8,128)(2,1)}), bf16[10240,128]{1,0:T(8,128)(2,1)}) %all-gather.14.cloned.1.call-update) | async-done | bytes 2621456 | tf_op jit(solution)/shard_map/all_gather | solution.py:176
  716.0 177.4 %while.15 = (s32[]{:T(128)}, f32[640,1,4]{0,2,1:T(4,128)S(1)}, f32[640,1,4]{0,2,1:T(4,128)S(1)}, f32[640,1,4,128]{0,3,2,1:T(8,128)}, s32[20]{0:T(128)S(1)}, /*in...) while((s32[]{:T(128)}, f32[640,1,4]{0,2,1:T(4,128)S(1)}, ...), condition=%wide.region_15.16_spmd.clone, body=%wide.region_12.15_spmd.clone.sunk | while | flops 690110592 | bytes 31246076 | solution.py:195
  721.0 2.8 fusion.100
  729.9 2.8 fusion.100
  738.8 2.8 fusion.100
  747.6 2.8 fusion.100
  (395 shorter events, 177.3 us)
Async XLA Ops:
  6.5 205.9 %all-gather.18.cloned.1.call-start = ((), (), s32[]{:S(2)}) async-start(), calls=%async_computation.6 | async-start | bytes 7925760 | tf_op jit(solution)/shard_map/all_gather | solution.py:96
  7.3 408.2 %all-gather.20.cloned.1.call-start = ((), (), s32[]{:S(2)}) async-start(), calls=%async_computation.7 | async-start | bytes 7925760 | tf_op jit(solution)/shard_map/all_gather | solution.py:97
  8.0 484.8 %all-gather.10.cloned.1.call-start = ((), (), s32[]{:S(2)}) async-start(), calls=%async_computation.2 | async-start | bytes 2949120 | tf_op jit(solution)/shard_map/all_gather | solution.py:103
  223.1 203.0 %copy-start.3 = (bf16[128,1280]{1,0:T(8,128)(2,1)S(1)}, bf16[128,1280]{1,0:T(8,128)(2,1)}, u32[]{:S(2)}) copy-start(bf16[128,1280]{1,0:T(8,128)(2,1)} %param.18) | copy-start | bytes 983044
  223.1 203.0 %copy-start.12 = (f32[1280]{0:T(1024)S(1)}, f32[1280]{0:T(1024)}, u32[]{:S(2)}) copy-start(f32[1280]{0:T(1024)} %param.20) | copy-start | bytes 15364
  223.1 203.0 %copy-start.13 = (f32[1280]{0:T(1024)S(1)}, f32[1280]{0:T(1024)}, u32[]{:S(2)}) copy-start(f32[1280]{0:T(1024)} %param.19) | copy-start | bytes 15364
  426.0 8.3 copy-start.7
  426.1 8.3 copy-start.8
  426.1 9.5 %copy-start.14 = (u32[128]{0:T(128)S(1)}, u32[128]{0:T(128)}, u32[]{:S(2)}) copy-start(u32[128]{0:T(128)} %constant.103) | copy-start | bytes 1540
  426.1 10.7 %copy-start.10 = (s32[1,4]{1,0:T(1,128)S(1)}, s32[1,4]{1,0:T(1,128)}, u32[]{:S(2)}) copy-start(s32[1,4]{1,0:T(1,128)} %param.32) | copy-start | bytes 52
  426.1 10.9 %copy-start.9 = (s32[1,4]{1,0:T(1,128)S(1)}, s32[1,4]{1,0:T(1,128)}, u32[]{:S(2)}) copy-start(s32[1,4]{1,0:T(1,128)} %param.33) | copy-start | bytes 52
  435.5 194.6 %all-gather.12.cloned.1.call-start = ((), (), s32[]{:S(2)}) async-start(), calls=%async_computation.3 | async-start | bytes 9437184 | tf_op jit(solution)/shard_map/all_gather | solution.py:135
  523.0 112.5 %copy-start.11 = (f32[8192]{0:T(1024)S(1)}, f32[8192]{0:T(1024)}, u32[]{:S(2)}) copy-start(f32[8192]{0:T(1024)} %param.26) | copy-start | bytes 98308
  527.2 9.7 %all-to-all-start = ((s32[16,1,32]{2,1,0:T(1,128)}), s32[16,1,32]{2,1,0:T(1,128)S(1)}, u32[]{:S(2)}, u32[]{:S(2)}) async-start(s32[16,1,32]{2,1,0:T(1,128)} %all_to_all.9), calls=%async_computation | async-start | bytes 16384 | tf_op jit(solution)/shard_map/all_to_all | solution.py:134
  533.3 146.0 %all-gather.16.cloned.1.call-start = ((), (), s32[]{:S(2)}) async-start(), calls=%async_computation.5 | async-start | bytes 2785280 | tf_op jit(solution)/shard_map/all_gather | solution.py:177
  630.2 5.8 copy-start
  635.9 8.8 copy-start.5
  640.6 5.6 copy-start.6
  645.6 70.4 %all-gather.14.cloned.1.call-start = ((), (), s32[]{:S(2)}) async-start(), calls=%async_computation.4 | async-start | bytes 2785280 | tf_op jit(solution)/shard_map/all_gather | solution.py:176
  717.6 3.4 copy-start.1
  726.5 3.4 copy-start.1
  735.3 3.4 copy-start.1
  753.1 3.4 copy-start.1
  770.8 3.4 copy-start.1
  (36 other events, 75.0 us)
Sparse Core Ops, SparseCore 0:
  9.1 203.3 all-gather.17
  214.2 201.2 all-gather.19
  435.7 57.0 all-gather.9
  523.1 107.0 all-gather.11
  645.7 33.5 all-gather.15
  680.9 35.0 all-gather.13
where the time goes:
time: 907 us; the launch traced here: 903 us
  waiting for transfers between devices  574 us (63%)
  matrix products  128 us (14%)
  local copies, waits for them, and re-layouts  74.6 us (8%)
  blocking collectives  45.3 us (5%)
  other arithmetic  44.9 us (5%)
  loops' own time  14.9 us (2%)
  between operations  14.5 us (2%)
    all_gather x1, waiting for transfers between devices, body(): lax.all_gather(up_weight, ('dp', 'ctx'), axis=0, tiled=True)  202 us
    all_gather x1, waiting for transfers between devices, body(): lax.all_gather(down_weight, ('dp', 'ctx'), axis=0, tiled=True)  192 us
    all_gather x1, waiting for transfers between devices, body(): lax.all_gather(got_rows.reshape(-1, merged.shape[1]), 'dp', axis=1, tiled...  90.5 us
    dot_general x20, matrix products, attend(): jnp.einsum('qkgt,tkd->qkgd', weights.astype(jnp.bfloat16), value_block, p...  55.7 us
    all_gather x1, waiting for transfers between devices, body(): lax.all_gather(merged_in, 'dp', axis=0, tiled=True)  44.6 us
    dot_general x20, matrix products, attend(): jnp.einsum('qkgd,tkd->qkgt', queries, key_block, preferred_element_type=j...  41.2 us
    all_gather x1, waiting for transfers between devices, body(): key_shard = lax.all_gather(key_rows, 'ctx', axis=0, tiled=True)  36.7 us
    reduce_sum x20, other arithmetic, attend(): row_total = row_total * rescale + jnp.sum(weights, axis=-1)  25.9 us
  transfers between devices with their start and end apart: 7, of which 7 were waited for; matrix products, arithmetic and copies ran while one was open for 4% of the time, Pallas kernels for 0%

commit v1 on v0

v1 whole, which is shorter than its diff:
```python
import math

import jax
import jax.numpy as jnp
import numpy as np
from jax import lax
from jax.experimental import pallas as pl
from jax.experimental.pallas import tpu as pltpu
from jax.sharding import Mesh
from jax.sharding import PartitionSpec as P

HEAD_DIM = 128
MOST = 16
SEQ = 640
REACH = 8
WINDOW = SEQ * (REACH + 1)
KEY_BLOCK = 512
PADDED = -(-WINDOW // KEY_BLOCK) * KEY_BLOCK
QUERY_BLOCK = 128
GROUP = 4
IMAGES = 512
CAPACITY = 32

MASKED_SCORE = -1e30
LOWEST_PEAK = -1e29
EPSILON = 1e-06
DP = ("yh", "x")
CTX = ("z", "yl", "c")


def layer_norm(rows_in, norm_gain, norm_bias):
    values = rows_in.astype(jnp.float32)
    center = values - jnp.mean(values, axis=-1, keepdims=True)
    spread = jnp.mean(center * center, axis=-1, keepdims=True)
    return (center * lax.rsqrt(spread + EPSILON) * norm_gain + norm_bias).astype(jnp.bfloat16)


def quick_gelu(values):
    return values * jax.nn.sigmoid(1.702 * values)


def row_positions(size_table, offset_table, row_count):
    image_ends = jnp.cumsum(size_table, axis=1, dtype=jnp.int32)
    image_starts = image_ends - size_table
    within = jnp.arange(row_count, dtype=jnp.int32)[None, :, None]
    inside = (within >= image_starts[:, None, :]) & (within < image_ends[:, None, :])
    placed = offset_table[:, None, :] - image_starts[:, None, :] + within
    return jnp.sum(jnp.where(inside, placed, 0), axis=2, dtype=jnp.int32)


def gather_by_exchange(block, axes, count):
    return lax.all_to_all(
        jnp.broadcast_to(block[None], (count,) + block.shape), axes, split_axis=0, concat_axis=0
    )


def swap(rows, axis):
    return lax.ppermute(rows, axis, [(0, 1), (1, 0)])


def attention_kernel(
    info,
    image_src,
    image_dst,
    image_len,
    query_ref,
    low_ref,
    image_ref,
    text_ref,
    out_ref,
    text_held,
    key_wide,
    value_wide,
    image_key,
    image_value,
    key_held,
    value_held,
    sem,
):
    window_start = pl.multiple_of(info[0], SEQ)
    query_offset = info[1]
    copy = pltpu.make_async_copy(text_ref.at[pl.ds(window_start, WINDOW), :], text_held, sem)
    copy.start()

    def widen_image(step, unused):
        rows = pl.ds(pl.multiple_of(step * 256, 256), 256)
        image_key[rows, :] = image_ref[rows, :HEAD_DIM].astype(jnp.float32)
        image_value[rows, :] = image_ref[rows, HEAD_DIM:].astype(jnp.float32)
        return unused

    lax.fori_loop(0, 16, widen_image, 0)
    copy.wait()

    def widen_text(step, unused):
        rows = pl.ds(pl.multiple_of(step * 320, 320), 320)
        key_wide[rows, :] = text_held[rows, :HEAD_DIM].astype(jnp.float32)
        value_wide[rows, :] = text_held[rows, HEAD_DIM:].astype(jnp.float32)
        return unused

    lax.fori_loop(0, WINDOW // 320, widen_text, 0)
    row_in = lax.broadcasted_iota(jnp.int32, (MOST, HEAD_DIM), 0)

    def place(image, unused):
        target = image_dst[image]

        @pl.when((target >= 0) & (target < WINDOW))
        def _():
            origin = image_src[image]
            taken = row_in < image_len[image]
            rows = pl.ds(target, MOST)
            key_wide[rows, :] = jnp.where(taken, image_key[pl.ds(origin, MOST), :], key_wide[rows, :])
            value_wide[rows, :] = jnp.where(
                taken, image_value[pl.ds(origin, MOST), :], value_wide[rows, :]
            )

        return unused

    lax.fori_loop(0, IMAGES, place, 0)

    def narrow(step, unused):
        rows = pl.ds(pl.multiple_of(step * 320, 320), 320)
        key_held[rows, :] = key_wide[rows, :].astype(jnp.bfloat16)
        value_held[rows, :] = value_wide[rows, :].astype(jnp.bfloat16)
        return unused

    lax.fori_loop(0, WINDOW // 320, narrow, 0)
    if PADDED > WINDOW:
        key_held[WINDOW:, :] = jnp.zeros((PADDED - WINDOW, HEAD_DIM), jnp.bfloat16)
        value_held[WINDOW:, :] = jnp.zeros((PADDED - WINDOW, HEAD_DIM), jnp.bfloat16)

    tall = GROUP * QUERY_BLOCK
    to_power = math.log2(math.e) / math.sqrt(HEAD_DIM)
    row_at = lax.broadcasted_iota(jnp.int32, (QUERY_BLOCK, 1), 0)

    def query_step(block, unused):
        rows = pl.ds(pl.multiple_of(block * QUERY_BLOCK, QUERY_BLOCK), QUERY_BLOCK)
        first = query_offset + block * QUERY_BLOCK
        queries = jnp.concatenate(
            [query_ref[rows, h * HEAD_DIM : (h + 1) * HEAD_DIM] for h in range(GROUP)], axis=0
        )
        low_rows = jnp.concatenate([low_ref[rows, :]] * GROUP, axis=0)
        high_rows = jnp.concatenate([row_at + first] * GROUP, axis=0)
        low_first = info[2 + 2 * block]
        low_last = info[3 + 2 * block]
        begin = low_first // KEY_BLOCK
        end = (first + QUERY_BLOCK - 1) // KEY_BLOCK + 1
        clear_begin = jnp.minimum((low_last + KEY_BLOCK - 1) // KEY_BLOCK, end)
        clear_end = jnp.maximum((first + 1) // KEY_BLOCK, clear_begin)

        def key_step(at, running, masked):
            peak, total, gathered = running
            keys_at = pl.ds(pl.multiple_of(at * KEY_BLOCK, KEY_BLOCK), KEY_BLOCK)
            scores = lax.dot_general(
                queries,
                key_held[keys_at, :],
                (((1,), (1,)), ((), ())),
                preferred_element_type=jnp.float32,
            )
            if masked:
                place_at = at * KEY_BLOCK + lax.broadcasted_iota(jnp.int32, (1, KEY_BLOCK), 1)
                scores = jnp.where(
                    (place_at >= low_rows) & (place_at <= high_rows), scores, MASKED_SCORE
                )
            new_peak = jnp.maximum(peak, jnp.max(scores, axis=-1, keepdims=True))
            weights = jnp.exp2((scores - new_peak) * to_power)
            rescale = jnp.exp2((peak - new_peak) * to_power)
            total = total * rescale + jnp.sum(weights, axis=-1, keepdims=True)
            gathered = gathered * rescale + jnp.dot(
                weights.astype(jnp.bfloat16),
                value_held[keys_at, :],
                preferred_element_type=jnp.float32,
            )
            return new_peak, total, gathered

        running = (
            jnp.full((tall, 1), LOWEST_PEAK, jnp.float32),
            jnp.zeros((tall, 1), jnp.float32),
            jnp.zeros((tall, HEAD_DIM), jnp.float32),
        )
        running = lax.fori_loop(begin, clear_begin, lambda a, r: key_step(a, r, True), running)
        running = lax.fori_loop(clear_begin, clear_end, lambda a, r: key_step(a, r, False), running)
        peak, total, gathered = lax.fori_loop(
            clear_end, end, lambda a, r: key_step(a, r, True), running
        )
        context = (gathered / total).astype(jnp.bfloat16)
        for h in range(GROUP):
            out_ref[rows, h * HEAD_DIM : (h + 1) * HEAD_DIM] = context[
                h * QUERY_BLOCK : (h + 1) * QUERY_BLOCK
            ]
        return unused

    lax.fori_loop(0, SEQ // QUERY_BLOCK, query_step, 0)


def attention(info, image_src, image_dst, image_len, queries, low_rows, image_kv, text_kv):
    smem = pl.BlockSpec(memory_space=pltpu.SMEM)
    vmem = pl.BlockSpec(memory_space=pltpu.VMEM)
    image_rows = image_kv.shape[0]
    return pl.pallas_call(
        attention_kernel,
        out_shape=jax.ShapeDtypeStruct(queries.shape, jnp.bfloat16),
        in_specs=[smem] * 4 + [vmem] * 3 + [pl.BlockSpec(memory_space=pl.ANY)],
        out_specs=vmem,
        scratch_shapes=[
            pltpu.VMEM((WINDOW, 2 * HEAD_DIM), jnp.bfloat16),
            pltpu.VMEM((WINDOW + MOST, HEAD_DIM), jnp.float32),
            pltpu.VMEM((WINDOW + MOST, HEAD_DIM), jnp.float32),
            pltpu.VMEM((image_rows + MOST, HEAD_DIM), jnp.float32),
            pltpu.VMEM((image_rows + MOST, HEAD_DIM), jnp.float32),
            pltpu.VMEM((PADDED, HEAD_DIM), jnp.bfloat16),
            pltpu.VMEM((PADDED, HEAD_DIM), jnp.bfloat16),
            pltpu.SemaphoreType.DMA,
        ],
        compiler_params=pltpu.CompilerParams(vmem_limit_bytes=48 * 1024 * 1024),
        cost_estimate=pl.CostEstimate(
            flops=8_000_000_000, bytes_accessed=8_000_000, transcendentals=13_000_000
        ),
    )(info, image_src, image_dst, image_len, queries, low_rows, image_kv, text_kv)


def body(
    patches,
    vision_gain,
    vision_bias,
    up_weight,
    down_weight,
    merge_gain,
    merge_bias,
    merge_weight,
    attn_gain,
    query_weight,
    kv_weight,
    text_query,
    text_kv,
    doc_ids,
    image_sizes,
    image_offsets,
):
    z_at, yl_at, c_at = lax.axis_index("z"), lax.axis_index("yl"), lax.axis_index("c")
    ctx_index = lax.axis_index(CTX)
    width = patches.shape[1]
    own_rows = patches.shape[0]

    text_window = lax.all_gather(
        jnp.concatenate([text_kv[0], text_kv[1]], axis=1), CTX, axis=0, tiled=True
    )
    below = jnp.sum(
        (doc_ids[:, None] < jnp.arange(4, dtype=jnp.int32)[None, :]).astype(jnp.int32),
        axis=0,
        dtype=jnp.int32,
    )
    facts = lax.all_gather(
        jnp.concatenate([image_sizes, image_offsets, below[None, :]], axis=1), DP + CTX, axis=0
    ).reshape(8, 16, 12)

    normed = layer_norm(patches, vision_gain, vision_bias)
    spare = ((0, 24 - up_weight.shape[0]), (0, 0))
    units = gather_by_exchange(
        jnp.concatenate([jnp.pad(up_weight, spare), jnp.pad(down_weight, spare)], axis=0),
        DP + ("z",),
        32,
    )
    ups = units[:, :24].reshape(-1, width)
    downs = units[:, 24:].reshape(-1, width)
    pair = jnp.concatenate([normed, swap(normed, "yl")], axis=0)
    four = jnp.concatenate([pair, swap(pair, "c")], axis=0)
    hidden = quick_gelu(
        lax.dot_general(four, ups, (((1,), (1,)), ((), ())), preferred_element_type=jnp.float32)
    ).astype(jnp.bfloat16)
    partial = jnp.dot(hidden, downs, preferred_element_type=jnp.float32)
    half = partial[: 2 * own_rows] + swap(
        partial[2 * own_rows :].astype(jnp.bfloat16), "c"
    ).astype(jnp.float32)
    branch = half[:own_rows] + swap(half[own_rows:].astype(jnp.bfloat16), "yl").astype(jnp.float32)
    vision = (patches.astype(jnp.float32) + branch).astype(jnp.bfloat16)
    merged_in = layer_norm(vision, merge_gain, merge_bias).reshape(-1, 4 * width)

    column_in = gather_by_exchange(merged_in, DP, 8).reshape(-1, 4 * width)
    merged = jnp.dot(column_in, merge_weight, preferred_element_type=jnp.float32).astype(
        jnp.bfloat16
    )
    whole = gather_by_exchange(merged, DP, 8)
    wide = whole.astype(jnp.float32)
    part = merged.shape[1]
    mean_square = jnp.sum(wide * wide, axis=(0, 2), keepdims=True) / (8 * part)
    ready = (wide * lax.rsqrt(mean_square + EPSILON) * attn_gain.reshape(8, 1, part)).astype(
        jnp.bfloat16
    )
    ready = jnp.swapaxes(ready, 0, 1).reshape(merged.shape[0], 8 * part)
    image_kv = jnp.concatenate(
        [
            jnp.dot(ready, kv_weight[0], preferred_element_type=jnp.float32),
            jnp.dot(ready, kv_weight[1], preferred_element_type=jnp.float32),
        ],
        axis=1,
    ).astype(jnp.bfloat16)
    image_query = jnp.dot(ready, query_weight, preferred_element_type=jnp.float32).astype(
        jnp.bfloat16
    )

    sizes = jnp.swapaxes(facts[:, :, :4], 0, 1)
    offsets = jnp.swapaxes(facts[:, :, 4:8], 0, 1)
    starts = jnp.sum(facts[0, :, 8:], axis=0, dtype=jnp.int32)
    positions = row_positions(sizes.reshape(128, 4), offsets.reshape(128, 4), CAPACITY).reshape(
        16, 256
    )
    before = jnp.arange(256)[None, :] < jnp.arange(256)[:, None]
    own_owner = lax.dynamic_index_in_dim(positions, ctx_index, 0, False) // SEQ
    own_rank = jnp.sum(
        ((own_owner[None, :] == own_owner[:, None]) & before).astype(jnp.int32),
        axis=1,
        dtype=jnp.int32,
    )
    own_slot = own_owner * CAPACITY + own_rank
    spread_out = (jnp.arange(512, dtype=jnp.int32)[:, None] == own_slot[None, :]).astype(
        jnp.bfloat16
    )
    mine = positions // SEQ == ctx_index
    rank = jnp.sum((mine[:, None, :] & before[None]).astype(jnp.int32), axis=2, dtype=jnp.int32)
    slot_here = mine[:, :, None] & (
        rank[:, :, None] == jnp.arange(CAPACITY, dtype=jnp.int32)[None, None, :]
    )
    slot_place = jnp.sum(
        jnp.where(slot_here, positions[:, :, None] - ctx_index * SEQ + 1, 0),
        axis=1,
        dtype=jnp.int32,
    ).reshape(-1) - 1
    bring_in = jnp.arange(SEQ, dtype=jnp.int32)[:, None] == slot_place[None, :]
    is_image = jnp.any(bring_in, axis=1)

    blocks = [image_kv]
    for step in (1, 2, 3):
        blocks.append(lax.ppermute(image_kv, "z", [(i, (i + step) % 4) for i in range(4)]))
    plane = jnp.concatenate(blocks, axis=0)
    plane = jnp.concatenate([plane, swap(plane, "yl")], axis=0)
    every_kv = jnp.concatenate([plane, swap(plane, "c")], axis=0)

    sent = jnp.dot(spread_out, image_query, preferred_element_type=jnp.float32).astype(jnp.bfloat16)
    got = lax.all_to_all(
        sent.reshape(16, CAPACITY, -1), CTX, split_axis=0, concat_axis=0
    ).reshape(512, -1)
    placed_query = jnp.dot(
        bring_in.astype(jnp.bfloat16), got, preferred_element_type=jnp.float32
    ).astype(jnp.bfloat16)
    queries = jnp.where(is_image[:, None], placed_query, text_query)

    window_start = jnp.maximum(ctx_index - REACH, 0) * SEQ
    low_rows = (
        jnp.sum(
            jnp.where(
                doc_ids[:, None] == jnp.arange(4, dtype=jnp.int32)[None, :], starts[None, :], 0
            ),
            axis=1,
            dtype=jnp.int32,
        )
        - window_start
    )
    low_rows = jnp.maximum(low_rows, 0)
    edges = low_rows.reshape(-1, QUERY_BLOCK)
    info = jnp.concatenate(
        [
            jnp.stack([window_start, ctx_index * SEQ - window_start]).astype(jnp.int32),
            jnp.stack([edges[:, 0], edges[:, -1]], axis=1).reshape(-1),
        ]
    )
    source = jnp.arange(16, dtype=jnp.int32)
    source_block = (
        ((source % 2) ^ c_at) * 8 + (((source // 2) % 2) ^ yl_at) * 4 + (z_at - source // 4 + 4) % 4
    )
    within_device = jnp.cumsum(sizes, axis=2, dtype=jnp.int32) - sizes
    image_src = (
        source_block[:, None, None] * 256
        + jnp.arange(8, dtype=jnp.int32)[None, :, None] * CAPACITY
        + within_device
    )
    return attention(
        info,
        image_src.reshape(-1),
        (offsets - window_start).reshape(-1),
        sizes.reshape(-1),
        queries,
        low_rows[:, None],
        every_kv,
        text_window,
    )


def solution(mesh):
    fine = Mesh(mesh.devices.reshape(2, 4, 4, 2, 2), DP + CTX)
    every = DP + CTX
    return jax.shard_map(
        body,
        mesh=fine,
        in_specs=(
            P(every, None),
            P(),
            P(),
            P(every, None),
            P(every, None),
            P(),
            P(),
            P(None, DP),
            P(),
            P(None, DP),
            P(None, None, DP),
            P(CTX, DP),
            P(None, CTX, DP),
            P(CTX),
            P(every, None),
            P(every, None),
        ),
        out_specs=P(CTX, DP),
        check_vma=False,
    )
```

time: 907 us -> 497 us (0.55)
  waiting for transfers between devices: 574 us -> 120 us
  blocking collectives: 45.3 us -> 214 us
  matrix products: 128 us -> 25 us
  local copies, waits for them, and re-layouts: 74.6 us -> 19.6 us
  Pallas kernels: 0 us -> 47.3 us
  starting transfers between devices: 6.38 us -> 42.5 us
  other arithmetic: 44.9 us -> 13.8 us
  loops' own time: 14.9 us -> 0 us
    all_gather x6 -> x1, waiting for transfers between devices: 569 us -> 0.02 us  [body(): lax.all_gather(jnp.concatenate([text_kv[0], text_kv[1]], axis=1), CTX, ax...]
    all_gather x1, blocking collectives: 16.5 us -> 214 us  [body(): lax.all_gather(jnp.concatenate([image_sizes, image_offsets, below[None, :...]
    dot_general x43 -> x5, matrix products: 120 us -> 18.2 us  [the longest x1 8.07 us: body(): jnp.dot(spread_out, image_query, preferred_element_type=jnp.float32)]
    ppermute x0 -> x9, waiting for transfers between devices: none -> 79.9 us  [the longest x6 73.5 us: swap(): return lax.ppermute(rows, axis, [(0, 1), (1, 0)])]
    pallas_call x0 -> x1, Pallas kernels: none -> 47.3 us  [attention(): pl.pallas_call(attention_kernel, out_shape=jax.ShapeDtypeStruct(queries.s...]
    all_to_all x1 -> x4, waiting for transfers between devices: 3.48 us -> 39.9 us  [the longest x3 33.1 us: gather_by_exchange(): lax.all_to_all(jnp.broadcast_to(block[None], (count,) + block.shape), axe...]
    reduce_sum x22 -> x7, other arithmetic: 31.2 us -> 4.75 us  [the longest x1 3.3 us: body(): mean_square = jnp.sum(wide * wide, axis=(0, 2), keepdims=True) / (8 * part)]
    all_to_all x1 -> x4, starting transfers between devices: 6.18 us -> 29.4 us  [the longest x3 23.5 us: gather_by_exchange(): lax.all_to_all(jnp.broadcast_to(block[None], (count,) + block.shape), axe...]
  transfers between devices with their start and end apart: 7 -> 14, of which waited for: 7 -> 9; matrix products, arithmetic and copies ran while one was open for 4% -> 9% of each run, Pallas kernels for 0% -> 0%
where the time goes in v1:
time: 497 us; the launch traced here: 496 us
  blocking collectives  214 us (43%)
  waiting for transfers between devices  120 us (24%)
  Pallas kernels  47.3 us (10%)
  starting transfers between devices  42.5 us (9%)
  matrix products  25 us (5%)
  local copies, waits for them, and re-layouts  19.6 us (4%)
  other arithmetic  13.8 us (3%)
  between operations  13.8 us (3%)
    all_gather x1, blocking collectives, body(): lax.all_gather(jnp.concatenate([image_sizes, image_offsets, below[None, :...  214 us
    ppermute x6, waiting for transfers between devices, swap(): return lax.ppermute(rows, axis, [(0, 1), (1, 0)])  73.5 us
    pallas_call x1, Pallas kernels, attention(): pl.pallas_call(attention_kernel, out_shape=jax.ShapeDtypeStruct(queries.s...  47.3 us
    all_to_all x3, waiting for transfers between devices, gather_by_exchange(): lax.all_to_all(jnp.broadcast_to(block[None], (count,) + block.shape), axe...  33.1 us
    all_to_all x3, starting transfers between devices, gather_by_exchange(): lax.all_to_all(jnp.broadcast_to(block[None], (count,) + block.shape), axe...  23.5 us
  transfers between devices with their start and end apart: 14, of which 9 were waited for; matrix products, arithmetic and copies ran while one was open for 9% of the time, Pallas kernels for 0%

profile of v1, /device:TPU:41, one launch (start us, length us, event | category | flops | bytes accessed | tf_op | source)
XLA Modules:
  0.0 495.9 jit_solution(11040732406524674694)
XLA Ops:
  7.4 2.2 broadcast_in_dim.42
  9.6 9.4 %all-to-all-start = ((bf16[32,48,1280]{2,1,0:T(8,128)(2,1)}), bf16[32,48,1280]{2,1,0:T(8,128)(2,1)}, u32[]{:S(2)}, u32[]{:S(2)}) async-start(bf16[32,48,1280]{2,1,0:T(8,128)(2,1)} %broadcast_in_dim.42), calls=%async_computation | async-start | bytes 7864320 | tf_op jit(solution)/shard_map/all_to_all | solution.py:52
  20.8 52.1 %collective-permute-done = bf16[128,1280]{1,0:T(8,128)(2,1)S(1)} collective-permute-done((bf16[128,1280]{1,0:T(8,128)(2,1)S(1)}, bf16[128,1280]{1,0:T(8,128)(2,1)S(1)}, u32[]{:S(2)}, u32[]{:S(2)}) %collective-permute-start) | collective-permute-done | bytes 327712 | tf_op jit(solution)/shard_map/ppermute | solution.py:58
  72.9 1.8 collective-permute-start.1
  74.8 3.7 fusion.72
  78.5 5.7 %fusion.27 = f32[512,1280]{1,0:T(8,128)} fusion(bf16[768,1280]{1,0:T(8,128)(2,1)} %bitcast.62, bf16[768,1280]{1,0:T(8,128)(2,1)S(1)} %bitcast.61, bf16[256,1280]{1,0:T(8,128)(2,1)} %collective-permute-done.1, bf16[128,1280]{1,0:T(8,128)(2,1)} %copy-done.3, bf16[128,1280]{1,0:T(8,128)(2,1)S(1)} %fusion.38), kind=kOutput, calls=%fused_computation.37 | convolution fusion | flops 2019557376 | bytes 7864320 | tf_op jit(solution)/shard_map/dot_general | solution.py:270
  89.8 8.9 %collective-permute-done.3 = bf16[128,1280]{1,0:T(8,128)(2,1)S(1)} collective-permute-done((bf16[128,1280]{1,0:T(8,128)(2,1)S(1)}, bf16[128,1280]{1,0:T(8,128)(2,1)S(1)}, u32[]{:S(2)}, u32[]{:S(2)}) %collective-permute-start.3) | collective-permute-done | bytes 327712 | tf_op jit(solution)/shard_map/ppermute | solution.py:58
  99.7 1.8 broadcast_in_dim.48
  101.5 7.9 %all-to-all-start.1 = ((bf16[8,32,5120]{2,1,0:T(8,128)(2,1)}), bf16[8,32,5120]{2,1,0:T(8,128)(2,1)S(1)}, u32[]{:S(2)}, u32[]{:S(2)}) async-start(bf16[8,32,5120]{2,1,0:T(8,128)(2,1)} %broadcast_in_dim.48), calls=%async_computation.1 | async-start | bytes 5242880 | tf_op jit(solution)/shard_map/all_to_all | solution.py:52
  110.4 33.1 %all-to-all-done.1 = bf16[8,32,5120]{2,1,0:T(8,128)(2,1)S(1)} async-done(((bf16[8,32,5120]{2,1,0:T(8,128)(2,1)}), bf16[8,32,5120]{2,1,0:T(8,128)(2,1)S(1)}, u32[]{:S(2)}, u32[]{:S(2)}) %all-to-all-start.1) | async-done | bytes 2621472 | tf_op jit(solution)/shard_map/all_to_all | solution.py:52
  143.5 6.8 %convolution_convert_fusion.1 = bf16[256,1024]{1,0:T(8,128)(2,1)S(1)} fusion(bf16[256,5120]{1,0:T(8,128)(2,1)S(1)} %bitcast.60, bf16[5120,1024]{1,0:T(8,128)(2,1)} %param.23), kind=kOutput, calls=%fused_computation.24 | convolution fusion | flops 2684616704 | bytes 13631488 | tf_op jit(solution)/shard_map/dot_general | solution.py:279
  150.6 2.3 broadcast_in_dim.49
  153.0 6.2 %all-to-all-start.2 = ((bf16[8,256,1024]{1,2,0:T(8,128)(2,1)}), bf16[8,256,1024]{1,2,0:T(8,128)(2,1)}, u32[]{:S(2)}, u32[]{:S(2)}) async-start(bf16[8,256,1024]{1,2,0:T(8,128)(2,1)} %broadcast_in_dim.49), calls=%async_computation.2 | async-start | bytes 8388608 | tf_op jit(solution)/shard_map/all_to_all | solution.py:52
  159.2 214.0 %all-gather.1 = s32[128,1,12]{2,1,0:T(1,128)S(1)} all-gather(s32[1,1,12]{2,1,0:T(1,128)S(1)} %add_bitcast_fusion), channel_id=2, replica_groups=mesh['yh'=2,'x'=4,'z'=4,'yl'=2,'c'=2] {'yh','x','z','yl','c'}, dimensions={0}, use_global_device_ids=true | all-gather | bytes 6192 | tf_op jit(solution)/shard_map/all_gather | solution.py:252
  375.9 3.3 fusion
  379.2 3.0 fusion.2
  386.3 7.5 %collective-permute-start.5 = (bf16[256,256]{1,0:T(8,128)(2,1)S(1)}, bf16[256,256]{1,0:T(8,128)(2,1)S(1)}, u32[]{:S(2)}, u32[]{:S(2)}) collective-permute-start(bf16[256,256]{1,0:T(8,128)(2,1)S(1)} %get-tuple-element.27), channel_id=1, source_target_pairs={{0,8},{4,12},{8,0},{12,4},{1,9},{5,13},{9,1},{13,5},{2,10},{6,14},... | collective-permute-start | bytes 393224 | tf_op jit(solution)/shard_map/ppermute | solution.py:333
  393.9 1.8 collective-permute-done.4
  397.2 3.2 collective-permute-done.6
  402.5 10.8 %collective-permute-done.7 = bf16[1024,256]{1,0:T(8,128)(2,1)S(1)} collective-permute-done((bf16[1024,256]{1,0:T(8,128)(2,1)S(1)}, bf16[1024,256]{1,0:T(8,128)(2,1)S(1)}, u32[]{:S(2)}, u32[]{:S(2)}) %collective-permute-start.7) | collective-permute-done | bytes 524320 | tf_op jit(solution)/shard_map/ppermute | solution.py:58
  415.7 8.1 %convolution_convert_fusion.2 = bf16[512,512]{1,0:T(8,128)(2,1)} fusion(bf16[256,8192]{0,1:T(8,128)(2,1)} %bitcast.59, bf16[8192,512]{1,0:T(8,128)(2,1)} %param.25, s32[256]{0:T(256)S(1)} %bitcast.70), kind=kOutput, calls=%fused_computation.25 | convolution fusion | flops 2282225664 | bytes 13108224 | tf_op jit(solution)/shard_map/dot_general | solution.py:338
  423.8 6.0 %all-to-all-start.3 = ((bf16[16,32,512]{2,1,0:T(8,128)(2,1)}), bf16[16,32,512]{2,1,0:T(8,128)(2,1)S(1)}, u32[]{:S(2)}, u32[]{:S(2)}) async-start(bf16[16,32,512]{2,1,0:T(8,128)(2,1)} %bitcast.17), calls=%async_computation.3 | async-start | bytes 1048576 | tf_op jit(solution)/shard_map/all_to_all | solution.py:339
  431.0 6.8 %all-to-all-done.3 = bf16[16,32,512]{2,1,0:T(8,128)(2,1)S(1)} async-done(((bf16[16,32,512]{2,1,0:T(8,128)(2,1)}), bf16[16,32,512]{2,1,0:T(8,128)(2,1)S(1)}, u32[]{:S(2)}, u32[]{:S(2)}) %all-to-all-start.3) | async-done | bytes 524320 | tf_op jit(solution)/shard_map/all_to_all | solution.py:339
  441.7 47.3 %shard_map.154 = bf16[640,512]{1,0:T(8,128)(2,1)} custom-call(s32[12]{0:T(128)S(1)} %pad_add_fusion.1.info, s32[512]{0:T(512)S(1)} %reshape.319.image_src, s32[512]{0:T(512)S(1)} %reshape.320.image_dst, s32[512]{0:T(512)S(1)} %reshape.321.image_len, bf16[640,512]{1,0:T(8,128)(2,1)S(1)} %fusion.16.query_ref, s32[640,1]{1,0:T(8,128)S(1)} %max.28.low_ref, ...), custom_call_target="tpu_custom_call" | custom-call | flops 8000000000 | bytes 8000000 | tf_op jit(solution)/shard_map/pallas_call | solution.py:199
  (122 shorter events, 28.4 us)
Async XLA Ops:
  9.6 9.4 %copy-start = (bf16[128,1280]{1,0:T(8,128)(2,1)S(1)}, bf16[128,1280]{1,0:T(8,128)(2,1)}, u32[]{:S(2)}) copy-start(bf16[128,1280]{1,0:T(8,128)(2,1)} %param.16) | copy-start | bytes 983044
  9.6 9.8 %copy-start.7 = (f32[1280]{0:T(1024)S(1)}, f32[1280]{0:T(1024)}, u32[]{:S(2)}) copy-start(f32[1280]{0:T(1024)} %param.18) | copy-start | bytes 15364
  9.6 9.8 %copy-start.8 = (f32[1280]{0:T(1024)S(1)}, f32[1280]{0:T(1024)}, u32[]{:S(2)}) copy-start(f32[1280]{0:T(1024)} %param.17) | copy-start | bytes 15364
  9.6 65.2 %all-to-all-start = ((bf16[32,48,1280]{2,1,0:T(8,128)(2,1)}), bf16[32,48,1280]{2,1,0:T(8,128)(2,1)}, u32[]{:S(2)}, u32[]{:S(2)}) async-start(bf16[32,48,1280]{2,1,0:T(8,128)(2,1)} %broadcast_in_dim.42), calls=%async_computation | async-start | bytes 7864320 | tf_op jit(solution)/shard_map/all_to_all | solution.py:52
  19.6 53.2 %collective-permute-start = (bf16[128,1280]{1,0:T(8,128)(2,1)S(1)}, bf16[128,1280]{1,0:T(8,128)(2,1)S(1)}, u32[]{:S(2)}, u32[]{:S(2)}) collective-permute-start(bf16[128,1280]{1,0:T(8,128)(2,1)S(1)} %fusion.38), channel_id=1, source_target_pairs={{0,2},{2,0},{1,3},{3,1},{4,6},{6,4},{5,7},{7,5},{8,10},{10,8},{9,1... | collective-permute-start | bytes 983048 | tf_op jit(solution)/shard_map/ppermute | solution.py:58
  72.9 5.5 %collective-permute-start.1 = (bf16[256,1280]{1,0:T(8,128)(2,1)S(1)}, bf16[256,1280]{1,0:T(8,128)(2,1)}, u32[]{:S(2)}, u32[]{:S(2)}) collective-permute-start(bf16[256,1280]{1,0:T(8,128)(2,1)S(1)} %pad_maximum_fusion), channel_id=1, source_target_pairs={{0,1},{1,0},{2,3},{3,2},{4,5},{5,4},{6,7},{7,6},{8,9},{9,8},{10,11... | collective-permute-start | bytes 1966088 | tf_op jit(solution)/shard_map/ppermute | solution.py:58
  85.6 2.6 collective-permute-start.2
  89.6 9.5 %copy-start.9 = (f32[1280]{0:T(1024)S(1)}, f32[1280]{0:T(1024)}, u32[]{:S(2)}) copy-start(f32[1280]{0:T(1024)} %param.22) | copy-start | bytes 15364
  89.6 9.5 %copy-start.10 = (f32[1280]{0:T(1024)S(1)}, f32[1280]{0:T(1024)}, u32[]{:S(2)}) copy-start(f32[1280]{0:T(1024)} %param.21) | copy-start | bytes 15364
  89.7 9.0 %collective-permute-start.3 = (bf16[128,1280]{1,0:T(8,128)(2,1)S(1)}, bf16[128,1280]{1,0:T(8,128)(2,1)S(1)}, u32[]{:S(2)}, u32[]{:S(2)}) collective-permute-start(bf16[128,1280]{1,0:T(8,128)(2,1)S(1)} %slice.95), channel_id=1, source_target_pairs={{0,2},{2,0},{1,3},{3,1},{4,6},{6,4},{5,7},{7,5},{8,10},{10,8},{9,1... | collective-permute-start | bytes 983048 | tf_op jit(solution)/shard_map/ppermute | solution.py:58
  101.5 8.0 %copy-start.4 = (bf16[2,640,128]{2,1,0:T(8,128)(2,1)S(1)}, bf16[2,640,128]{2,1,0:T(8,128)(2,1)}, u32[]{:S(2)}) copy-start(bf16[2,640,128]{2,1,0:T(8,128)(2,1)} %param.28) | copy-start | bytes 983044
  101.5 8.8 %copy-start.6 = (s32[640]{0:T(1024)S(1)}, s32[640]{0:T(1024)}, u32[]{:S(2)}) copy-start(s32[640]{0:T(1024)} %param.29) | copy-start | bytes 7684
  101.5 42.1 %all-to-all-start.1 = ((bf16[8,32,5120]{2,1,0:T(8,128)(2,1)}), bf16[8,32,5120]{2,1,0:T(8,128)(2,1)S(1)}, u32[]{:S(2)}, u32[]{:S(2)}) async-start(bf16[8,32,5120]{2,1,0:T(8,128)(2,1)} %broadcast_in_dim.48), calls=%async_computation.1 | async-start | bytes 5242880 | tf_op jit(solution)/shard_map/all_to_all | solution.py:52
  109.4 332.3 %all-gather.4.cloned.1.call-start = ((), (), s32[]{:S(2)}) async-start(), calls=%async_computation.4 | async-start | bytes 5570560 | tf_op jit(solution)/shard_map/all_gather | solution.py:244
  152.9 6.2 %copy-start.11 = (s32[1,4]{1,0:T(1,128)S(1)}, s32[1,4]{1,0:T(1,128)}, u32[]{:S(2)}) copy-start(s32[1,4]{1,0:T(1,128)} %param.31) | copy-start | bytes 52
  152.9 6.2 %copy-start.12 = (s32[1,4]{1,0:T(1,128)S(1)}, s32[1,4]{1,0:T(1,128)}, u32[]{:S(2)}) copy-start(s32[1,4]{1,0:T(1,128)} %param.30) | copy-start | bytes 52
  153.0 220.5 %copy-start.5 = (f32[8192]{0:T(1024)S(1)}, f32[8192]{0:T(1024)}, u32[]{:S(2)}) copy-start(f32[8192]{0:T(1024)} %param.24) | copy-start | bytes 98308
  153.0 223.0 %all-to-all-start.2 = ((bf16[8,256,1024]{1,2,0:T(8,128)(2,1)}), bf16[8,256,1024]{1,2,0:T(8,128)(2,1)}, u32[]{:S(2)}, u32[]{:S(2)}) async-start(bf16[8,256,1024]{1,2,0:T(8,128)(2,1)} %broadcast_in_dim.49), calls=%async_computation.2 | async-start | bytes 8388608 | tf_op jit(solution)/shard_map/all_to_all | solution.py:52
  386.2 9.5 %collective-permute-start.4 = (bf16[256,256]{1,0:T(8,128)(2,1)S(1)}, bf16[256,256]{1,0:T(8,128)(2,1)S(1)}, u32[]{:S(2)}, u32[]{:S(2)}) collective-permute-start(bf16[256,256]{1,0:T(8,128)(2,1)S(1)} %get-tuple-element.27), channel_id=1, source_target_pairs={{0,4},{4,8},{8,12},{12,0},{1,5},{5,9},{9,13},{13,1},{2,6},{6,10},{... | collective-permute-start | bytes 393224 | tf_op jit(solution)/shard_map/ppermute | solution.py:333
  386.3 10.9 %collective-permute-start.5 = (bf16[256,256]{1,0:T(8,128)(2,1)S(1)}, bf16[256,256]{1,0:T(8,128)(2,1)S(1)}, u32[]{:S(2)}, u32[]{:S(2)}) collective-permute-start(bf16[256,256]{1,0:T(8,128)(2,1)S(1)} %get-tuple-element.27), channel_id=1, source_target_pairs={{0,8},{4,12},{8,0},{12,4},{1,9},{5,13},{9,1},{13,5},{2,10},{6,14},... | collective-permute-start | bytes 393224 | tf_op jit(solution)/shard_map/ppermute | solution.py:333
  393.7 6.6 %collective-permute-start.6 = (bf16[256,256]{1,0:T(8,128)(2,1)S(1)}, bf16[256,256]{1,0:T(8,128)(2,1)S(1)}, u32[]{:S(2)}, u32[]{:S(2)}) collective-permute-start(bf16[256,256]{1,0:T(8,128)(2,1)S(1)} %get-tuple-element.27), channel_id=1, source_target_pairs={{0,12},{4,0},{8,4},{12,8},{1,13},{5,1},{9,5},{13,9},{2,14},{6,2},{... | collective-permute-start | bytes 393224 | tf_op jit(solution)/shard_map/ppermute | solution.py:333
  400.4 12.9 %collective-permute-start.7 = (bf16[1024,256]{1,0:T(8,128)(2,1)S(1)}, bf16[1024,256]{1,0:T(8,128)(2,1)S(1)}, u32[]{:S(2)}, u32[]{:S(2)}) collective-permute-start(bf16[1024,256]{1,0:T(8,128)(2,1)S(1)} %pad_maximum_fusion.1), channel_id=1, source_target_pairs={{0,2},{2,0},{1,3},{3,1},{4,6},{6,4},{5,7},{7,5},{8,10},{10,8},{9,1... | collective-permute-start | bytes 1572872 | tf_op jit(solution)/shard_map/ppermute | solution.py:58
  414.2 26.2 %collective-permute-start.8 = (bf16[2048,256]{1,0:T(8,128)(2,1)}, bf16[2048,256]{1,0:T(8,128)(2,1)}, u32[]{:S(2)}, u32[]{:S(2)}) collective-permute-start(bf16[2048,256]{1,0:T(8,128)(2,1)} %get-tuple-element.15), channel_id=1, source_target_pairs={{0,1},{1,0},{2,3},{3,2},{4,5},{5,4},{6,7},{7,6},{8,9},{9,8},{10,11... | collective-permute-start | bytes 3145736 | tf_op jit(solution)/shard_map/ppermute | solution.py:58
  423.8 14.0 %all-to-all-start.3 = ((bf16[16,32,512]{2,1,0:T(8,128)(2,1)}), bf16[16,32,512]{2,1,0:T(8,128)(2,1)S(1)}, u32[]{:S(2)}, u32[]{:S(2)}) async-start(bf16[16,32,512]{2,1,0:T(8,128)(2,1)} %bitcast.17), calls=%async_computation.3 | async-start | bytes 1048576 | tf_op jit(solution)/shard_map/all_to_all | solution.py:339
  (4 other events, 8.2 us)
Sparse Core Ops, SparseCore 0:
  111.9 57.6 all-gather.3

commit v2 on v1

--- a/solution.py
+++ b/solution.py
@@ -20,6 +20,9 @@
 GROUP = 4
 IMAGES = 512
 CAPACITY = 32
+CHUNK = 16
+CTX_COUNT = 16
+DP_COUNT = 8
 
 MASKED_SCORE = -1e30
 LOWEST_PEAK = -1e29
@@ -63,9 +66,11 @@
     image_src,
     image_dst,
     image_len,
-    query_ref,
+    text_query_ref,
+    bring_ref,
     low_ref,
-    image_ref,
+    first_ref,
+    last_ref,
     text_ref,
     out_ref,
     text_held,
@@ -73,6 +78,7 @@
     value_wide,
     image_key,
     image_value,
+    image_query,
     key_held,
     value_held,
     sem,
@@ -82,13 +88,25 @@
     copy = pltpu.make_async_copy(text_ref.at[pl.ds(window_start, WINDOW), :], text_held, sem)
     copy.start()
 
-    def widen_image(step, unused):
-        rows = pl.ds(pl.multiple_of(step * 256, 256), 256)
-        image_key[rows, :] = image_ref[rows, :HEAD_DIM].astype(jnp.float32)
-        image_value[rows, :] = image_ref[rows, HEAD_DIM:].astype(jnp.float32)
+    def widen_image(source, unused):
+        for device in range(DP_COUNT):
+            base = source * (DP_COUNT * CAPACITY) + device * CAPACITY
+            rows = pl.ds(pl.multiple_of(base, CHUNK), CHUNK)
+            block = first_ref[source, device * CHUNK : (device + 1) * CHUNK, :].astype(jnp.float32)
+            image_key[rows, :] = block[:, :HEAD_DIM]
+            image_value[rows, :] = block[:, HEAD_DIM:]
+            rows = pl.ds(pl.multiple_of(base + CHUNK, CHUNK), CHUNK)
+            at, side = device % 4 * CHUNK, device // 4 * 2 * HEAD_DIM
+            block = last_ref[source, at : at + CHUNK, side : side + 2 * HEAD_DIM].astype(
+                jnp.float32
+            )
+            image_key[rows, :] = block[:, :HEAD_DIM]
+            image_value[rows, :] = block[:, HEAD_DIM:]
+        rows = pl.ds(pl.multiple_of(source * CAPACITY, CAPACITY), CAPACITY)
+        image_query[rows, :] = last_ref[source, 4 * CHUNK :, :]
         return unused
 
-    lax.fori_loop(0, 16, widen_image, 0)
+    lax.fori_loop(0, CTX_COUNT, widen_image, 0)
     copy.wait()
 
     def widen_text(step, unused):
@@ -135,8 +153,15 @@
     def query_step(block, unused):
         rows = pl.ds(pl.multiple_of(block * QUERY_BLOCK, QUERY_BLOCK), QUERY_BLOCK)
         first = query_offset + block * QUERY_BLOCK
+        bring = bring_ref[rows, :]
+        is_image = jnp.max(bring.astype(jnp.float32), axis=-1, keepdims=True) > 0.5
+        placed = jnp.where(
+            is_image,
+            jnp.dot(bring, image_query[...], preferred_element_type=jnp.float32),
+            text_query_ref[rows, :].astype(jnp.float32),
+        ).astype(jnp.bfloat16)
         queries = jnp.concatenate(
-            [query_ref[rows, h * HEAD_DIM : (h + 1) * HEAD_DIM] for h in range(GROUP)], axis=0
+            [placed[:, h * HEAD_DIM : (h + 1) * HEAD_DIM] for h in range(GROUP)], axis=0
         )
         low_rows = jnp.concatenate([low_ref[rows, :]] * GROUP, axis=0)
         high_rows = jnp.concatenate([row_at + first] * GROUP, axis=0)
@@ -192,14 +217,14 @@
     lax.fori_loop(0, SEQ // QUERY_BLOCK, query_step, 0)
 
 
-def attention(info, image_src, image_dst, image_len, queries, low_rows, image_kv, text_kv):
+def attention(info, image_src, image_dst, image_len, text_query, bring_in, low_rows, first, last, text):
     smem = pl.BlockSpec(memory_space=pltpu.SMEM)
     vmem = pl.BlockSpec(memory_space=pltpu.VMEM)
-    image_rows = image_kv.shape[0]
+    image_rows = CTX_COUNT * DP_COUNT * CAPACITY
     return pl.pallas_call(
         attention_kernel,
-        out_shape=jax.ShapeDtypeStruct(queries.shape, jnp.bfloat16),
-        in_specs=[smem] * 4 + [vmem] * 3 + [pl.BlockSpec(memory_space=pl.ANY)],
+        out_shape=jax.ShapeDtypeStruct(text_query.shape, jnp.bfloat16),
+        in_specs=[smem] * 4 + [vmem] * 5 + [pl.BlockSpec(memory_space=pl.ANY)],
         out_specs=vmem,
         scratch_shapes=[
             pltpu.VMEM((WINDOW, 2 * HEAD_DIM), jnp.bfloat16),
@@ -207,6 +232,7 @@
             pltpu.VMEM((WINDOW + MOST, HEAD_DIM), jnp.float32),
             pltpu.VMEM((image_rows + MOST, HEAD_DIM), jnp.float32),
             pltpu.VMEM((image_rows + MOST, HEAD_DIM), jnp.float32),
+            pltpu.VMEM((CTX_COUNT * CAPACITY, GROUP * HEAD_DIM), jnp.bfloat16),
             pltpu.VMEM((PADDED, HEAD_DIM), jnp.bfloat16),
             pltpu.VMEM((PADDED, HEAD_DIM), jnp.bfloat16),
             pltpu.SemaphoreType.DMA,
@@ -215,7 +241,7 @@
         cost_estimate=pl.CostEstimate(
             flops=8_000_000_000, bytes_accessed=8_000_000, transcendentals=13_000_000
         ),
-    )(info, image_src, image_dst, image_len, queries, low_rows, image_kv, text_kv)
+    )(info, image_src, image_dst, image_len, text_query, bring_in, low_rows, first, last, text)
 
 
 def body(
@@ -236,7 +262,6 @@
     image_sizes,
     image_offsets,
 ):
-    z_at, yl_at, c_at = lax.axis_index("z"), lax.axis_index("yl"), lax.axis_index("c")
     ctx_index = lax.axis_index(CTX)
     width = patches.shape[1]
     own_rows = patches.shape[0]
@@ -249,54 +274,71 @@
         axis=0,
         dtype=jnp.int32,
     )
-    facts = lax.all_gather(
-        jnp.concatenate([image_sizes, image_offsets, below[None, :]], axis=1), DP + CTX, axis=0
-    ).reshape(8, 16, 12)
-
-    normed = layer_norm(patches, vision_gain, vision_bias)
+    facts = gather_by_exchange(
+        jnp.concatenate([image_sizes, image_offsets, below[None, :]], axis=1), DP + ("yl",), 16
+    )
+    facts = gather_by_exchange(facts.reshape(16, 12), ("z", "c"), 8)
+    facts = facts.reshape(4, 2, 8, 2, 12).transpose(2, 0, 3, 1, 4).reshape(8, 16, 12)
+
     spare = ((0, 24 - up_weight.shape[0]), (0, 0))
     units = gather_by_exchange(
         jnp.concatenate([jnp.pad(up_weight, spare), jnp.pad(down_weight, spare)], axis=0),
-        DP + ("z",),
-        32,
-    )
+        DP + ("yl",),
+        16,
+    )
+    normed = layer_norm(patches, vision_gain, vision_bias)
+    column = gather_by_exchange(normed, ("z",), 4).reshape(-1, width)
+    near_rows = column.shape[0]
+    near = jnp.concatenate([column, swap(column, "c")], axis=0)
     ups = units[:, :24].reshape(-1, width)
     downs = units[:, 24:].reshape(-1, width)
-    pair = jnp.concatenate([normed, swap(normed, "yl")], axis=0)
-    four = jnp.concatenate([pair, swap(pair, "c")], axis=0)
     hidden = quick_gelu(
-        lax.dot_general(four, ups, (((1,), (1,)), ((), ())), preferred_element_type=jnp.float32)
+        lax.dot_general(near, ups, (((1,), (1,)), ((), ())), preferred_element_type=jnp.float32)
     ).astype(jnp.bfloat16)
-    partial = jnp.dot(hidden, downs, preferred_element_type=jnp.float32)
-    half = partial[: 2 * own_rows] + swap(
-        partial[2 * own_rows :].astype(jnp.bfloat16), "c"
-    ).astype(jnp.float32)
-    branch = half[:own_rows] + swap(half[own_rows:].astype(jnp.bfloat16), "yl").astype(jnp.float32)
+    away = jnp.dot(hidden[near_rows:], downs, preferred_element_type=jnp.float32).astype(
+        jnp.bfloat16
+    )
+    here = jnp.dot(hidden[:near_rows], downs, preferred_element_type=jnp.float32)
+    pair_sum = (here + swap(away, "c").astype(jnp.float32)).astype(jnp.bfloat16)
+    terms = lax.all_to_all(
+        pair_sum.reshape(4, own_rows, width), "z", split_axis=0, concat_axis=0
+    )
+    branch = jnp.sum(terms.astype(jnp.float32), axis=0)
     vision = (patches.astype(jnp.float32) + branch).astype(jnp.bfloat16)
     merged_in = layer_norm(vision, merge_gain, merge_bias).reshape(-1, 4 * width)
 
-    column_in = gather_by_exchange(merged_in, DP, 8).reshape(-1, 4 * width)
-    merged = jnp.dot(column_in, merge_weight, preferred_element_type=jnp.float32).astype(
-        jnp.bfloat16
-    )
-    whole = gather_by_exchange(merged, DP, 8)
-    wide = whole.astype(jnp.float32)
-    part = merged.shape[1]
-    mean_square = jnp.sum(wide * wide, axis=(0, 2), keepdims=True) / (8 * part)
-    ready = (wide * lax.rsqrt(mean_square + EPSILON) * attn_gain.reshape(8, 1, part)).astype(
-        jnp.bfloat16
-    )
-    ready = jnp.swapaxes(ready, 0, 1).reshape(merged.shape[0], 8 * part)
-    image_kv = jnp.concatenate(
-        [
-            jnp.dot(ready, kv_weight[0], preferred_element_type=jnp.float32),
-            jnp.dot(ready, kv_weight[1], preferred_element_type=jnp.float32),
-        ],
-        axis=1,
-    ).astype(jnp.bfloat16)
-    image_query = jnp.dot(ready, query_weight, preferred_element_type=jnp.float32).astype(
-        jnp.bfloat16
-    )
+    columns = [
+        gather_by_exchange(merged_in[at : at + CHUNK], DP, DP_COUNT).reshape(-1, 4 * width)
+        for at in (0, CHUNK)
+    ]
+    wholes = []
+    for column_in in columns:
+        merged = jnp.dot(column_in, merge_weight, preferred_element_type=jnp.float32).astype(
+            jnp.bfloat16
+        )
+        wholes.append(gather_by_exchange(merged, DP, DP_COUNT))
+    image_kvs, image_queries = [], []
+    for whole in wholes:
+        wide = whole.astype(jnp.float32)
+        part = whole.shape[2]
+        mean_square = jnp.sum(wide * wide, axis=(0, 2), keepdims=True) / (DP_COUNT * part)
+        ready = (wide * lax.rsqrt(mean_square + EPSILON) * attn_gain.reshape(8, 1, part)).astype(
+            jnp.bfloat16
+        )
+        ready = jnp.swapaxes(ready, 0, 1).reshape(whole.shape[1], DP_COUNT * part)
+        image_kvs.append(
+            jnp.concatenate(
+                [
+                    jnp.dot(ready, kv_weight[0], preferred_element_type=jnp.float32),
+                    jnp.dot(ready, kv_weight[1], preferred_element_type=jnp.float32),
+                ],
+                axis=1,
+            ).astype(jnp.bfloat16)
+        )
+        image_queries.append(
+            jnp.dot(ready, query_weight, preferred_element_type=jnp.float32).astype(jnp.bfloat16)
+        )
+    first = gather_by_exchange(image_kvs[0], CTX, CTX_COUNT)
 
     sizes = jnp.swapaxes(facts[:, :, :4], 0, 1)
     offsets = jnp.swapaxes(facts[:, :, 4:8], 0, 1)
@@ -311,7 +353,7 @@
         axis=1,
         dtype=jnp.int32,
     )
-    own_slot = own_owner * CAPACITY + own_rank
+    own_slot = (own_owner * CAPACITY + own_rank).reshape(8, 2, CHUNK).swapaxes(0, 1).reshape(-1)
     spread_out = (jnp.arange(512, dtype=jnp.int32)[:, None] == own_slot[None, :]).astype(
         jnp.bfloat16
     )
@@ -326,23 +368,30 @@
         dtype=jnp.int32,
     ).reshape(-1) - 1
     bring_in = jnp.arange(SEQ, dtype=jnp.int32)[:, None] == slot_place[None, :]
-    is_image = jnp.any(bring_in, axis=1)
-
-    blocks = [image_kv]
-    for step in (1, 2, 3):
-        blocks.append(lax.ppermute(image_kv, "z", [(i, (i + step) % 4) for i in range(4)]))
-    plane = jnp.concatenate(blocks, axis=0)
-    plane = jnp.concatenate([plane, swap(plane, "yl")], axis=0)
-    every_kv = jnp.concatenate([plane, swap(plane, "c")], axis=0)
-
-    sent = jnp.dot(spread_out, image_query, preferred_element_type=jnp.float32).astype(jnp.bfloat16)
-    got = lax.all_to_all(
-        sent.reshape(16, CAPACITY, -1), CTX, split_axis=0, concat_axis=0
-    ).reshape(512, -1)
-    placed_query = jnp.dot(
-        bring_in.astype(jnp.bfloat16), got, preferred_element_type=jnp.float32
+
+    chunk_rows = DP_COUNT * CHUNK
+    sent = sum(
+        jnp.dot(
+            spread_out[:, k * chunk_rows : (k + 1) * chunk_rows],
+            image_queries[k],
+            preferred_element_type=jnp.float32,
+        )
+        for k in (0, 1)
     ).astype(jnp.bfloat16)
-    queries = jnp.where(is_image[:, None], placed_query, text_query)
+    half = chunk_rows // 2
+    folded = jnp.concatenate([image_kvs[1][:half], image_kvs[1][half:]], axis=1)
+    last = lax.all_to_all(
+        jnp.concatenate(
+            [
+                jnp.broadcast_to(folded[None], (CTX_COUNT,) + folded.shape),
+                sent.reshape(CTX_COUNT, CAPACITY, -1),
+            ],
+            axis=1,
+        ),
+        CTX,
+        split_axis=0,
+        concat_axis=0,
+    )
 
     window_start = jnp.maximum(ctx_index - REACH, 0) * SEQ
     low_rows = (
@@ -363,14 +412,9 @@
             jnp.stack([edges[:, 0], edges[:, -1]], axis=1).reshape(-1),
         ]
     )
-    source = jnp.arange(16, dtype=jnp.int32)
-    source_block = (
-        ((source % 2) ^ c_at) * 8 + (((source // 2) % 2) ^ yl_at) * 4 + (z_at - source // 4 + 4) % 4
-    )
     within_device = jnp.cumsum(sizes, axis=2, dtype=jnp.int32) - sizes
     image_src = (
-        source_block[:, None, None] * 256
-        + jnp.arange(8, dtype=jnp.int32)[None, :, None] * CAPACITY
+        jnp.arange(CTX_COUNT * DP_COUNT, dtype=jnp.int32).reshape(CTX_COUNT, DP_COUNT, 1) * CAPACITY
         + within_device
     )
     return attention(
@@ -378,9 +422,11 @@
         image_src.reshape(-1),
         (offsets - window_start).reshape(-1),
         sizes.reshape(-1),
-        queries,
+        text_query,
+        bring_in.astype(jnp.bfloat16),
         low_rows[:, None],
-        every_kv,
+        first,
+        last,
         text_window,
     )
 

time: 497 us -> 360 us (0.72)
  the two profiles are of different devices: /device:TPU:41 before, /device:TPU:72 now
where the time goes in v2:
time: 360 us; the launch traced here: 353 us
  waiting for transfers between devices  135 us (38%)
  starting transfers between devices  63.3 us (18%)
  Pallas kernels  43.1 us (12%)
  matrix products  36.1 us (10%)
  other arithmetic  32.5 us (9%)
  local copies, waits for them, and re-layouts  29.6 us (8%)
  between operations  13.9 us (4%)
    all_to_all x9, waiting for transfers between devices, gather_by_exchange(): lax.all_to_all(jnp.broadcast_to(block[None], (count,) + block.shape), axe...  103 us
    all_to_all x9, starting transfers between devices, gather_by_exchange(): lax.all_to_all(jnp.broadcast_to(block[None], (count,) + block.shape), axe...  51.7 us
    pallas_call x1, Pallas kernels, attention(): pl.pallas_call(attention_kernel, out_shape=jax.ShapeDtypeStruct(text_quer...  43.1 us
    all_to_all x1, waiting for transfers between devices, body(): lax.all_to_all(jnp.concatenate([jnp.broadcast_to(folded[None], (CTX_COUNT...  17.7 us
    all_to_all x1, waiting for transfers between devices, body(): lax.all_to_all(pair_sum.reshape(4, own_rows, width), 'z', split_axis=0, c...  13.7 us
    dot_general x2, matrix products, body(): jnp.dot(spread_out[:, k * chunk_rows:(k + 1) * chunk_rows], image_queries...  12.7 us
    dot_general x2, matrix products, body(): jnp.dot(column_in, merge_weight, preferred_element_type=jnp.float32)  11.7 us
    broadcast_in_dim x11, local copies, waits for them, and re-layouts, gather_by_exchange(): jnp.broadcast_to(block[None], (count,) + block.shape)  10.3 us
  transfers between devices with their start and end apart: 14, of which 10 were waited for; matrix products, arithmetic and copies ran while one was open for 23% of the time, Pallas kernels for 0%

profile of v2, /device:TPU:72, one launch (start us, length us, event | category | flops | bytes accessed | tf_op | source)
XLA Modules:
  0.0 353.1 jit_solution(14150174174157258203)
XLA Ops:
  11.3 5.0 %all-to-all-start.2 = ((bf16[4,128,1280]{2,1,0:T(8,128)(2,1)}), bf16[4,128,1280]{2,1,0:T(8,128)(2,1)S(1)}, u32[]{:S(2)}, u32[]{:S(2)}) async-start(bf16[4,128,1280]{2,1,0:T(8,128)(2,1)} %broadcast_in_dim.60), calls=%async_computation.2 | async-start | bytes 2621440 | tf_op jit(solution)/shard_map/all_to_all | solution.py:55
  16.3 14.9 %all-to-all-done.2 = bf16[4,128,1280]{2,1,0:T(8,128)(2,1)S(1)} async-done(((bf16[4,128,1280]{2,1,0:T(8,128)(2,1)}), bf16[4,128,1280]{2,1,0:T(8,128)(2,1)S(1)}, u32[]{:S(2)}, u32[]{:S(2)}) %all-to-all-start.2) | async-done | bytes 1310752 | tf_op jit(solution)/shard_map/all_to_all | solution.py:55
  32.9 7.4 %all-to-all-start.3 = ((bf16[16,48,1280]{2,1,0:T(8,128)(2,1)}), bf16[16,48,1280]{2,1,0:T(8,128)(2,1)S(1)}, u32[]{:S(2)}, u32[]{:S(2)}) async-start(bf16[16,48,1280]{2,1,0:T(8,128)(2,1)} %broadcast_in_dim.61), calls=%async_computation.3 | async-start | bytes 3932160 | tf_op jit(solution)/shard_map/all_to_all | solution.py:55
  40.3 26.4 %all-to-all-done.3 = bf16[16,48,1280]{2,1,0:T(8,128)(2,1)S(1)} async-done(((bf16[16,48,1280]{2,1,0:T(8,128)(2,1)}), bf16[16,48,1280]{2,1,0:T(8,128)(2,1)S(1)}, u32[]{:S(2)}, u32[]{:S(2)}) %all-to-all-start.3) | async-done | bytes 1966112 | tf_op jit(solution)/shard_map/all_to_all | solution.py:55
  73.8 4.7 %all-to-all-start = ((s32[16,1,12]{2,1,0:T(1,128)}), s32[16,1,12]{2,1,0:T(1,128)S(1)}, u32[]{:S(2)}, u32[]{:S(2)}) async-start(s32[16,1,12]{2,1,0:T(1,128)} %broadcast_in_dim.51), calls=%async_computation | async-start | bytes 16384 | tf_op jit(solution)/shard_map/all_to_all | solution.py:55
  80.5 4.3 %all-to-all-done = s32[16,1,12]{2,1,0:T(1,128)S(1)} async-done(((s32[16,1,12]{2,1,0:T(1,128)}), s32[16,1,12]{2,1,0:T(1,128)S(1)}, u32[]{:S(2)}, u32[]{:S(2)}) %all-to-all-start) | async-done | bytes 800 | tf_op jit(solution)/shard_map/all_to_all | solution.py:55
  84.8 5.7 %all-to-all-start.4 = ((bf16[4,128,1280]{2,1,0:T(8,128)(2,1)}), bf16[4,128,1280]{2,1,0:T(8,128)(2,1)S(1)}, u32[]{:S(2)}, u32[]{:S(2)}) async-start(bf16[4,128,1280]{2,1,0:T(8,128)(2,1)} %bitcast.16), calls=%async_computation.4 | async-start | bytes 2621440 | tf_op jit(solution)/shard_map/all_to_all | solution.py:303
  91.2 13.7 %all-to-all-done.4 = bf16[4,128,1280]{2,1,0:T(8,128)(2,1)S(1)} async-done(((bf16[4,128,1280]{2,1,0:T(8,128)(2,1)}), bf16[4,128,1280]{2,1,0:T(8,128)(2,1)S(1)}, u32[]{:S(2)}, u32[]{:S(2)}) %all-to-all-start.4) | async-done | bytes 1310752 | tf_op jit(solution)/shard_map/all_to_all | solution.py:303
  104.9 6.2 %all-to-all-start.1 = ((s32[8,1,192]{2,1,0:T(1,128)}), s32[8,1,192]{2,1,0:T(1,128)S(1)}, u32[]{:S(2)}, u32[]{:S(2)}) async-start(s32[8,1,192]{2,1,0:T(1,128)} %reshape.334), calls=%async_computation.1 | async-start | bytes 16384 | tf_op jit(solution)/shard_map/all_to_all | solution.py:55
  119.0 20.1 %all-to-all-done.8 = bf16[8,16,5120]{2,1,0:T(8,128)(2,1)S(1)} async-done(((bf16[8,16,5120]{2,1,0:T(8,128)(2,1)}), bf16[8,16,5120]{2,1,0:T(8,128)(2,1)S(1)}, u32[]{:S(2)}, u32[]{:S(2)}) %all-to-all-start.8) | async-done | bytes 1310752 | tf_op jit(solution)/shard_map/all_to_all | solution.py:55
  148.1 5.5 %convolution_convert_fusion.1 = bf16[128,1024]{1,0:T(8,128)(2,1)S(1)} fusion(bf16[128,5120]{1,0:T(8,128)(2,1)S(1)} %bitcast.79, bf16[5120,1024]{1,0:T(8,128)(2,1)} %param.23), kind=kOutput, calls=%fused_computation.36 | convolution fusion | flops 1342308352 | bytes 12058624 | tf_op jit(solution)/shard_map/dot_general | solution.py:316
  153.8 10.3 %all-to-all-done.5 = bf16[8,16,5120]{2,1,0:T(8,128)(2,1)S(1)} async-done(((bf16[8,16,5120]{2,1,0:T(8,128)(2,1)}), bf16[8,16,5120]{2,1,0:T(8,128)(2,1)S(1)}, u32[]{:S(2)}, u32[]{:S(2)}) %all-to-all-start.5) | async-done | bytes 1310752 | tf_op jit(solution)/shard_map/all_to_all | solution.py:55
  183.4 6.2 %convolution_convert_fusion.2 = bf16[128,1024]{1,0:T(8,128)(2,1)} fusion(bf16[128,5120]{1,0:T(8,128)(2,1)S(1)} %bitcast.78, bf16[5120,1024]{1,0:T(8,128)(2,1)} %param.23), kind=kOutput, calls=%fused_computation.37 | convolution fusion | flops 1342308352 | bytes 12058624 | tf_op jit(solution)/shard_map/dot_general | solution.py:316
  190.7 7.2 %all-to-all-done.9 = bf16[8,128,1024]{1,2,0:T(8,128)(2,1)S(1)} async-done(((bf16[8,128,1024]{1,2,0:T(8,128)(2,1)}), bf16[8,128,1024]{1,2,0:T(8,128)(2,1)S(1)}, u32[]{:S(2)}, u32[]{:S(2)}) %all-to-all-start.9) | async-done | bytes 2097184 | tf_op jit(solution)/shard_map/all_to_all | solution.py:55
  199.6 6.6 %all-to-all-start.6 = ((bf16[8,128,1024]{1,2,0:T(8,128)(2,1)}), bf16[8,128,1024]{1,2,0:T(8,128)(2,1)}, u32[]{:S(2)}, u32[]{:S(2)}) async-start(bf16[8,128,1024]{1,2,0:T(8,128)(2,1)} %broadcast_in_dim.64), calls=%async_computation.6 | async-start | bytes 4194304 | tf_op jit(solution)/shard_map/all_to_all | solution.py:55
  206.2 6.1 %reduce_window_sum.22 = s32[16,8,4]{2,1,0:T(8,128)} reduce-window(s32[16,8,4]{2,1,0:T(8,128)S(1)} %get-tuple-element.21, s32[]{:T(128)} %constant.62.clone.1), window={size=1x1x4 pad=0_0x0_0x3_0}, to_apply=%region_3.4 | reduce-window | flops 1536 | bytes 4100 | tf_op jit(solution)/shard_map/jit(cumsum)/reduce_window_sum | solution.py:415
  215.6 18.0 %all-to-all-done.6 = bf16[8,128,1024]{1,2,0:T(8,128)(2,1)} async-done(((bf16[8,128,1024]{1,2,0:T(8,128)(2,1)}), bf16[8,128,1024]{1,2,0:T(8,128)(2,1)}, u32[]{:S(2)}, u32[]{:S(2)}) %all-to-all-start.6) | async-done | bytes 2097184 | tf_op jit(solution)/shard_map/all_to_all | solution.py:55
  236.4 4.4 %fusion.5 = (bf16[8,128,1024]{1,2,0:T(8,128)(2,1)}, bf16[8,128,1024]{1,2,0:T(8,128)(2,1)S(1)}) fusion(bf16[8,128,1024]{1,2,0:T(8,128)(2,1)S(1)} %all-to-all-done.9, f32[128]{0:T(128)S(1)} %add_rsqrt_fusion, f32[8,1024]{1,0:T(8,128)S(1)} %copy-done.11, f32[128]{0:T(128)S(1)} %add_rsqrt_fusion.1, bf16[8,128,1024]{1,2,0:T(8,128)(2,1)} %all-to-all-done.6), kind=kLoop, calls=%fused_computation.9 | loop fusion | flops 8388608 | bytes 8422400 | tf_op jit(solution)/shard_map/convert_element_type | solution.py:325
  244.1 10.9 %all-to-all-start.7 = ((bf16[16,128,256]{2,1,0:T(8,128)(2,1)}), bf16[16,128,256]{2,1,0:T(8,128)(2,1)S(1)}, u32[]{:S(2)}, u32[]{:S(2)}) async-start(bf16[16,128,256]{2,1,0:T(8,128)(2,1)} %broadcast_in_dim.65), calls=%async_computation.7 | async-start | bytes 2097152 | tf_op jit(solution)/shard_map/all_to_all | solution.py:55
  258.7 6.6 %fusion.24 = f32[512,512]{1,0:T(8,128)} fusion(bf16[128,8192]{0,1:T(8,128)(2,1)} %bitcast.87, bf16[8192,512]{1,0:T(8,128)(2,1)} %param.25, pred[512,256]{1,0:T(32,128)(4,1)S(1)} %copy-done.7), kind=kOutput, calls=%fused_computation.40 | convolution fusion | flops 1140916224 | bytes 11599872 | tf_op jit(solution)/shard_map/dot_general | solution.py:374
  267.1 6.1 %fusion.23 = bf16[512,512]{1,0:T(8,128)(2,1)} fusion(f32[512,512]{1,0:T(8,128)} %fusion.24, bf16[128,8192]{0,1:T(8,128)(2,1)S(1)} %bitcast.84, bf16[8192,512]{1,0:T(8,128)(2,1)} %param.25, pred[512,256]{1,0:T(32,128)(4,1)S(1)} %copy-done.7), kind=kOutput, calls=%fused_computation.35 | convolution fusion | flops 1141440512 | bytes 12124160 | tf_op jit(solution)/shard_map/dot_general | solution.py:374
  275.7 5.9 %all-to-all-start.10 = ((bf16[16,96,512]{2,1,0:T(8,128)(2,1)}), bf16[16,96,512]{2,1,0:T(8,128)(2,1)S(1)}, u32[]{:S(2)}, u32[]{:S(2)}) async-start(bf16[16,96,512]{2,1,0:T(8,128)(2,1)} %pad_maximum_fusion), calls=%async_computation.10 | async-start | bytes 3145728 | tf_op jit(solution)/shard_map/all_to_all | solution.py:383
  283.4 17.7 %all-to-all-done.10.last_ref = bf16[16,96,512]{2,1,0:T(8,128)(2,1)S(1)} async-done(((bf16[16,96,512]{2,1,0:T(8,128)(2,1)}), bf16[16,96,512]{2,1,0:T(8,128)(2,1)S(1)}, u32[]{:S(2)}, u32[]{:S(2)}) %all-to-all-start.10) | async-done | bytes 1572896 | tf_op jit(solution)/shard_map/all_to_all | solution.py:383
  303.1 43.1 %shard_map.154 = bf16[640,512]{1,0:T(8,128)(2,1)} custom-call(s32[12]{0:T(128)S(1)} %pad_add_fusion.1.info, s32[512]{0:T(512)S(1)} %reshape.306.image_src, s32[512]{0:T(512)S(1)} %reshape.307.image_dst, s32[512]{0:T(512)S(1)} %reshape.308.image_len, bf16[640,512]{1,0:T(8,128)(2,1)S(1)} %copy-done.1, bf16[640,512]{1,0:T(8,128)(2,1)S(1)} %fusion.22.bring_ref, ...), custom_call_target="tpu_custom_call" | custom-call | flops 8000000000 | bytes 8000000 | tf_op jit(solution)/shard_map/pallas_call | solution.py:224
  (166 shorter events, 76.1 us)
Async XLA Ops:
  11.3 19.9 %all-to-all-start.2 = ((bf16[4,128,1280]{2,1,0:T(8,128)(2,1)}), bf16[4,128,1280]{2,1,0:T(8,128)(2,1)S(1)}, u32[]{:S(2)}, u32[]{:S(2)}) async-start(bf16[4,128,1280]{2,1,0:T(8,128)(2,1)} %broadcast_in_dim.60), calls=%async_computation.2 | async-start | bytes 2621440 | tf_op jit(solution)/shard_map/all_to_all | solution.py:55
  32.9 33.8 %all-to-all-start.3 = ((bf16[16,48,1280]{2,1,0:T(8,128)(2,1)}), bf16[16,48,1280]{2,1,0:T(8,128)(2,1)S(1)}, u32[]{:S(2)}, u32[]{:S(2)}) async-start(bf16[16,48,1280]{2,1,0:T(8,128)(2,1)} %broadcast_in_dim.61), calls=%async_computation.3 | async-start | bytes 3932160 | tf_op jit(solution)/shard_map/all_to_all | solution.py:55
  40.3 26.6 %collective-permute-start = (bf16[512,1280]{1,0:T(8,128)(2,1)}, bf16[512,1280]{1,0:T(8,128)(2,1)}, u32[]{:S(2)}, u32[]{:S(2)}) collective-permute-start(bf16[512,1280]{1,0:T(8,128)(2,1)} %bitcast.92), channel_id=1, source_target_pairs={{0,1},{1,0},{2,3},{3,2},{4,5},{5,4},{6,7},{7,6},{8,9},{9,8},{10,11... | collective-permute-start | bytes 3932168 | tf_op jit(solution)/shard_map/ppermute | solution.py:61
  73.0 5.5 %collective-permute-start.1 = (bf16[512,1280]{1,0:T(8,128)(2,1)}, bf16[512,1280]{1,0:T(8,128)(2,1)S(1)}, u32[]{:S(2)}, u32[]{:S(2)}) collective-permute-start(bf16[512,1280]{1,0:T(8,128)(2,1)} %convolution_convert_fusion), channel_id=1, source_target_pairs={{0,1},{1,0},{2,3},{3,2},{4,5},{5,4},{6,7},{7,6},{8,9},{9,8},{10,11... | collective-permute-start | bytes 3932168 | tf_op jit(solution)/shard_map/ppermute | solution.py:61
  73.8 10.9 %all-to-all-start = ((s32[16,1,12]{2,1,0:T(1,128)}), s32[16,1,12]{2,1,0:T(1,128)S(1)}, u32[]{:S(2)}, u32[]{:S(2)}) async-start(s32[16,1,12]{2,1,0:T(1,128)} %broadcast_in_dim.51), calls=%async_computation | async-start | bytes 16384 | tf_op jit(solution)/shard_map/all_to_all | solution.py:55
  84.8 26.6 %copy-start.4 = (bf16[128,1280]{1,0:T(8,128)(2,1)S(1)}, bf16[128,1280]{1,0:T(8,128)(2,1)}, u32[]{:S(2)}) copy-start(bf16[128,1280]{1,0:T(8,128)(2,1)} %param.16) | copy-start | bytes 983044
  84.8 20.2 %all-to-all-start.4 = ((bf16[4,128,1280]{2,1,0:T(8,128)(2,1)}), bf16[4,128,1280]{2,1,0:T(8,128)(2,1)S(1)}, u32[]{:S(2)}, u32[]{:S(2)}) async-start(bf16[4,128,1280]{2,1,0:T(8,128)(2,1)} %bitcast.16), calls=%async_computation.4 | async-start | bytes 2621440 | tf_op jit(solution)/shard_map/all_to_all | solution.py:303
  90.5 21.3 %copy-start.22 = (f32[1280]{0:T(1024)S(1)}, f32[1280]{0:T(1024)}, u32[]{:S(2)}) copy-start(f32[1280]{0:T(1024)} %param.22) | copy-start | bytes 15364
  90.5 21.3 %copy-start.23 = (f32[1280]{0:T(1024)S(1)}, f32[1280]{0:T(1024)}, u32[]{:S(2)}) copy-start(f32[1280]{0:T(1024)} %param.21) | copy-start | bytes 15364
  104.9 9.2 %all-to-all-start.1 = ((s32[8,1,192]{2,1,0:T(1,128)}), s32[8,1,192]{2,1,0:T(1,128)S(1)}, u32[]{:S(2)}, u32[]{:S(2)}) async-start(s32[8,1,192]{2,1,0:T(1,128)} %reshape.334), calls=%async_computation.1 | async-start | bytes 16384 | tf_op jit(solution)/shard_map/all_to_all | solution.py:55
  115.3 23.8 %all-to-all-start.8 = ((bf16[8,16,5120]{2,1,0:T(8,128)(2,1)}), bf16[8,16,5120]{2,1,0:T(8,128)(2,1)S(1)}, u32[]{:S(2)}, u32[]{:S(2)}) async-start(bf16[8,16,5120]{2,1,0:T(8,128)(2,1)} %broadcast_in_dim.67), calls=%async_computation.8 | async-start | bytes 2621440 | tf_op jit(solution)/shard_map/all_to_all | solution.py:55
  119.0 25.1 %copy-start.8 = (bf16[2,640,128]{2,1,0:T(8,128)(2,1)S(1)}, bf16[2,640,128]{2,1,0:T(8,128)(2,1)}, u32[]{:S(2)}) copy-start(bf16[2,640,128]{2,1,0:T(8,128)(2,1)} %param.28) | copy-start | bytes 983044
  140.3 23.8 %all-to-all-start.5 = ((bf16[8,16,5120]{2,1,0:T(8,128)(2,1)}), bf16[8,16,5120]{2,1,0:T(8,128)(2,1)S(1)}, u32[]{:S(2)}, u32[]{:S(2)}) async-start(bf16[8,16,5120]{2,1,0:T(8,128)(2,1)} %broadcast_in_dim.63), calls=%async_computation.5 | async-start | bytes 2621440 | tf_op jit(solution)/shard_map/all_to_all | solution.py:55
  144.1 157.0 %all-gather.2.cloned.1.call-start = ((), (), s32[]{:S(2)}) async-start(), calls=%async_computation.11 | async-start | bytes 5570560 | tf_op jit(solution)/shard_map/all_gather | solution.py:269
  165.8 32.1 %all-to-all-start.9 = ((bf16[8,128,1024]{1,2,0:T(8,128)(2,1)}), bf16[8,128,1024]{1,2,0:T(8,128)(2,1)S(1)}, u32[]{:S(2)}, u32[]{:S(2)}) async-start(bf16[8,128,1024]{1,2,0:T(8,128)(2,1)} %broadcast_in_dim.72), calls=%async_computation.9 | async-start | bytes 4194304 | tf_op jit(solution)/shard_map/all_to_all | solution.py:55
  199.6 6.6 %copy-start.14 = (s32[8,2,16]{2,1,0:T(2,128)S(1)}, s32[8,2,16]{2,1,0:T(2,128)}, u32[]{:S(2)}) copy-start(s32[8,2,16]{2,1,0:T(2,128)} %reduce_sum.142) | copy-start | bytes 3076
  199.6 6.6 %copy-start.15 = (s32[8,2,16]{2,1,0:T(2,128)S(1)}, s32[8,2,16]{2,1,0:T(2,128)}, u32[]{:S(2)}) copy-start(s32[8,2,16]{2,1,0:T(2,128)} %div.62) | copy-start | bytes 3076
  199.6 6.6 %copy-start.19 = (pred[8,2,16]{2,1,0:T(4,128)(4,1)S(1)}, pred[8,2,16]{2,1,0:T(4,128)(4,1)}, u32[]{:S(2)}) copy-start(pred[8,2,16]{2,1,0:T(4,128)(4,1)} %and.66) | copy-start | bytes 772
  199.6 13.0 %copy-start.9 = (pred[256,256]{1,0:T(8,128)(4,1)S(1)}, pred[256,256]{1,0:T(8,128)(4,1)}, u32[]{:S(2)}) copy-start(pred[256,256]{1,0:T(8,128)(4,1)} %iota_compare_fusion.3) | copy-start | bytes 196612
  199.6 34.1 %all-to-all-start.6 = ((bf16[8,128,1024]{1,2,0:T(8,128)(2,1)}), bf16[8,128,1024]{1,2,0:T(8,128)(2,1)}, u32[]{:S(2)}, u32[]{:S(2)}) async-start(bf16[8,128,1024]{1,2,0:T(8,128)(2,1)} %broadcast_in_dim.64), calls=%async_computation.6 | async-start | bytes 4194304 | tf_op jit(solution)/shard_map/all_to_all | solution.py:55
  214.5 21.8 %copy-start.11 = (f32[8,1024]{1,0:T(8,128)S(1)}, f32[8,1024]{1,0:T(8,128)}, u32[]{:S(2)}) copy-start(f32[8,1024]{1,0:T(8,128)} %mul.138) | copy-start | bytes 98308
  242.9 12.1 %copy-start.2 = (bf16[8,128,1024]{1,2,0:T(8,128)(2,1)S(1)}, bf16[8,128,1024]{1,2,0:T(8,128)(2,1)}, u32[]{:S(2)}) copy-start(bf16[8,128,1024]{1,2,0:T(8,128)(2,1)} %get-tuple-element.24) | copy-start | bytes 6291460
  244.1 31.6 %all-to-all-start.7 = ((bf16[16,128,256]{2,1,0:T(8,128)(2,1)}), bf16[16,128,256]{2,1,0:T(8,128)(2,1)S(1)}, u32[]{:S(2)}, u32[]{:S(2)}) async-start(bf16[16,128,256]{2,1,0:T(8,128)(2,1)} %broadcast_in_dim.65), calls=%async_computation.7 | async-start | bytes 2097152 | tf_op jit(solution)/shard_map/all_to_all | solution.py:55
  275.7 25.4 %all-to-all-start.10 = ((bf16[16,96,512]{2,1,0:T(8,128)(2,1)}), bf16[16,96,512]{2,1,0:T(8,128)(2,1)S(1)}, u32[]{:S(2)}, u32[]{:S(2)}) async-start(bf16[16,96,512]{2,1,0:T(8,128)(2,1)} %pad_maximum_fusion), calls=%async_computation.10 | async-start | bytes 3145728 | tf_op jit(solution)/shard_map/all_to_all | solution.py:383
  (18 other events, 56.9 us)
Sparse Core Ops, SparseCore 0:
  146.6 64.7 all-gather.1
